TPU v7x, 128 devices: a whole 4x4x4 slice. The times are simulated.
128 devices in a mesh: row: 16 (over z, y_lo, core), col: 8 (over x, y_hi).
Axes of the slice: x: 4, y: 4 (y_hi: 2, y_lo: 2; y = y_hi * 2 + y_lo), z: 4, core: 2. Of those that a mesh axis runs over, the one named last changes fastest.
Arguments:
- amplitudes: bfloat16 [80, 80, 128, 128], P('row'), may hold values from -6 to 6
- integrals: bfloat16 [80, 80, 128, 128], P('row', 'col'), may hold values from -0.078125 to 0.078125
- pair_lists: int32 [80, 80, 48], P('row', 'col'), may hold values from 0 to 79, as said below
- pair_counts: int32 [80, 80], P('row', 'col'), may hold values from 24 to 48, as said below
Outputs:
- residual: float32 [80, 80, 128, 128], P('row', 'col')
Inputs may be any that keep to these rules, and one draw needn't show every extreme that they name: `pair_lists`: the 48 entries of each pair's list are distinct. `pair_counts`: every diagonal pair (i, i) keeps all 48 entries.
All inputs are finite; a program needn't handle non-finite values.
Results may differ from a plain program's by a relative error of at most 0.0003.
Values may be sent and summed in bfloat16 or wider, within the bound.
A program may use at most 64 MiB of HBM per device.

v0:
```python
import jax
import jax.numpy as jnp
from jax import lax
from jax.sharding import PartitionSpec as P


def shifted(value, axis, steps):
    count = lax.axis_size(axis)
    pairs = [(source, (source + steps) % count) for source in range(count)]
    return lax.ppermute(value, axis, pairs)


def on_device(amplitudes, integrals, pair_lists, pair_counts):
    rows_here = amplitudes.shape[0]
    kblock = integrals.shape[0]
    cols_here = integrals.shape[1]
    tile_size = integrals.shape[2]
    row_count = lax.axis_size("row")
    my_row = lax.axis_index("row")
    slot_ids = jnp.arange(pair_lists.shape[2], dtype=jnp.int32)
    in_count = slot_ids[None, None, :] < pair_counts[:, :, None]
    zero_total = jnp.zeros((rows_here, cols_here, tile_size, tile_size), jnp.float32)

    def contribute(total, integral_block, block_id):
        first_k = block_id * kblock
        k_labels = first_k + jnp.arange(kblock, dtype=jnp.int32)
        matches = (pair_lists[:, :, :, None] == k_labels[None, None, None, :]) & in_count[
            :, :, :, None
        ]
        alive_mask = jnp.any(matches, axis=2).astype(jnp.bfloat16)
        amp_piece = lax.dynamic_slice_in_dim(amplitudes, first_k, kblock, 1)
        masked = amp_piece[:, None, :, :, :] * alive_mask[:, :, :, None, None]
        return total + jnp.einsum(
            "ijkac,kjcb->ijab", masked, integral_block, preferred_element_type=jnp.float32
        )

    def advance(shift_count, loop_state):
        total, integral_block = loop_state
        total = contribute(total, integral_block, (my_row - shift_count) % row_count)
        integral_block = shifted(integral_block, "row", 1)
        return (total, integral_block)

    total, integral_block = lax.fori_loop(0, row_count - 1, advance, (zero_total, integrals))
    contracted = contribute(total, integral_block, (my_row - (row_count - 1)) % row_count)
    section_one = lax.all_to_all(contracted, "col", split_axis=2, concat_axis=1, tiled=True)
    mirrored = lax.all_to_all(
        lax.all_to_all(section_one, "row", split_axis=1, concat_axis=0, tiled=True),
        "col",
        split_axis=0,
        concat_axis=2,
        tiled=True,
    )
    return contracted + jnp.transpose(mirrored, (1, 0, 3, 2))


def solution(mesh):
    placed = (
        P("row", None, None, None),
        P("row", "col", None, None),
        P("row", "col", None),
        P("row", "col"),
    )
    return jax.shard_map(
        on_device,
        mesh=mesh,
        in_specs=placed,
        out_specs=P("row", "col", None, None),
        check_vma=False,
    )
```

profile of v0, /device:TPU:28, one launch (start us, length us, event | category | flops | bytes accessed | tf_op | source)
XLA Modules:
  0.0 511.6 jit_solution(5711380151575805801)
XLA Ops:
  6.7 320.2 %while.18 = (s32[]{:T(128)}, f32[5,10,128,128]{3,2,0,1:T(8,128)}, bf16[5,10,128,128]{3,2,0,1:T(8,128)(2,1)S(1)}, s32[]{:T(128)}, bf16[5,80,128,128]{3,2,1,0:T(8,...) while((s32[]{:T(128)}, f32[5,10,128,128]{3,2,0,1:T(8,128)}, ...), condition=%wide.region_2.3_spmd.clone, body=%wide.region_0.2_spmd.clone.sunk | while | flops 1054348800 | bytes 20497988 | solution.py:43
  13.4 14.0 %collective-permute-done = bf16[5,10,128,128]{3,2,0,1:T(8,128)(2,1)S(1)} collective-permute-done((bf16[5,10,128,128]{3,2,0,1:T(8,128)(2,1)S(1)}, bf16[5,10,128,128]{3,2,0,1:T(8,128)(2,1)S(1)}, u32[]{:S(2)}, u32[]{:S(2)}) %collective-permute-start) | collective-permute-done | bytes 1638432 | tf_op jit(solution)/shard_map/while/body/eval_jaxpr/ppermute | solution.py:10
  35.5 12.6 %collective-permute-done = bf16[5,10,128,128]{3,2,0,1:T(8,128)(2,1)S(1)} collective-permute-done((bf16[5,10,128,128]{3,2,0,1:T(8,128)(2,1)S(1)}, bf16[5,10,128,128]{3,2,0,1:T(8,128)(2,1)S(1)}, u32[]{:S(2)}, u32[]{:S(2)}) %collective-permute-start) | collective-permute-done | bytes 1638432 | tf_op jit(solution)/shard_map/while/body/eval_jaxpr/ppermute | solution.py:10
  56.8 12.0 %collective-permute-done = bf16[5,10,128,128]{3,2,0,1:T(8,128)(2,1)S(1)} collective-permute-done((bf16[5,10,128,128]{3,2,0,1:T(8,128)(2,1)S(1)}, bf16[5,10,128,128]{3,2,0,1:T(8,128)(2,1)S(1)}, u32[]{:S(2)}, u32[]{:S(2)}) %collective-permute-start) | collective-permute-done | bytes 1638432 | tf_op jit(solution)/shard_map/while/body/eval_jaxpr/ppermute | solution.py:10
  78.4 11.2 %collective-permute-done = bf16[5,10,128,128]{3,2,0,1:T(8,128)(2,1)S(1)} collective-permute-done((bf16[5,10,128,128]{3,2,0,1:T(8,128)(2,1)S(1)}, bf16[5,10,128,128]{3,2,0,1:T(8,128)(2,1)S(1)}, u32[]{:S(2)}, u32[]{:S(2)}) %collective-permute-start) | collective-permute-done | bytes 1638432 | tf_op jit(solution)/shard_map/while/body/eval_jaxpr/ppermute | solution.py:10
  94.8 5.2 %bitcast_add_fusion.4 = f32[5,10,128,128]{3,2,0,1:T(8,128)} fusion(f32[5,10,128,128]{3,2,0,1:T(8,128)} %get-tuple-element.325, bf16[5,10,5]{2,0,1:T(8,128)(2,1)S(1)} %copy.76, bf16[5,5,128,128]{3,2,1,0:T(8,128)(2,1)S(1)} %constant_dynamic-slice_fusion.3, bf16[5,10,128,128]{3,2,0,1:T(8,128)(2,1)S(1)} %copy.82, pred[]{:T(512)S(6)} %compare.5), kind=kOutput, calls=%fused_computation.5.clone.1 | convolution fusion | flops 1054310400 | bytes 9011701 | tf_op jit(solution)/shard_map/while/body/eval_jaxpr/ijkac,kjcb->ijab/dot_general | solution.py:33
  100.1 10.3 %collective-permute-done = bf16[5,10,128,128]{3,2,0,1:T(8,128)(2,1)S(1)} collective-permute-done((bf16[5,10,128,128]{3,2,0,1:T(8,128)(2,1)S(1)}, bf16[5,10,128,128]{3,2,0,1:T(8,128)(2,1)S(1)}, u32[]{:S(2)}, u32[]{:S(2)}) %collective-permute-start) | collective-permute-done | bytes 1638432 | tf_op jit(solution)/shard_map/while/body/eval_jaxpr/ppermute | solution.py:10
  116.4 5.2 %bitcast_add_fusion.4 = f32[5,10,128,128]{3,2,0,1:T(8,128)} fusion(f32[5,10,128,128]{3,2,0,1:T(8,128)} %get-tuple-element.325, bf16[5,10,5]{2,0,1:T(8,128)(2,1)S(1)} %copy.76, bf16[5,5,128,128]{3,2,1,0:T(8,128)(2,1)S(1)} %constant_dynamic-slice_fusion.3, bf16[5,10,128,128]{3,2,0,1:T(8,128)(2,1)S(1)} %copy.82, pred[]{:T(512)S(6)} %compare.5), kind=kOutput, calls=%fused_computation.5.clone.1 | convolution fusion | flops 1054310400 | bytes 9011701 | tf_op jit(solution)/shard_map/while/body/eval_jaxpr/ijkac,kjcb->ijab/dot_general | solution.py:33
  121.7 9.3 %collective-permute-done = bf16[5,10,128,128]{3,2,0,1:T(8,128)(2,1)S(1)} collective-permute-done((bf16[5,10,128,128]{3,2,0,1:T(8,128)(2,1)S(1)}, bf16[5,10,128,128]{3,2,0,1:T(8,128)(2,1)S(1)}, u32[]{:S(2)}, u32[]{:S(2)}) %collective-permute-start) | collective-permute-done | bytes 1638432 | tf_op jit(solution)/shard_map/while/body/eval_jaxpr/ppermute | solution.py:10
  138.1 5.2 %bitcast_add_fusion.4 = f32[5,10,128,128]{3,2,0,1:T(8,128)} fusion(f32[5,10,128,128]{3,2,0,1:T(8,128)} %get-tuple-element.325, bf16[5,10,5]{2,0,1:T(8,128)(2,1)S(1)} %copy.76, bf16[5,5,128,128]{3,2,1,0:T(8,128)(2,1)S(1)} %constant_dynamic-slice_fusion.3, bf16[5,10,128,128]{3,2,0,1:T(8,128)(2,1)S(1)} %copy.82, pred[]{:T(512)S(6)} %compare.5), kind=kOutput, calls=%fused_computation.5.clone.1 | convolution fusion | flops 1054310400 | bytes 9011701 | tf_op jit(solution)/shard_map/while/body/eval_jaxpr/ijkac,kjcb->ijab/dot_general | solution.py:33
  143.3 8.4 %collective-permute-done = bf16[5,10,128,128]{3,2,0,1:T(8,128)(2,1)S(1)} collective-permute-done((bf16[5,10,128,128]{3,2,0,1:T(8,128)(2,1)S(1)}, bf16[5,10,128,128]{3,2,0,1:T(8,128)(2,1)S(1)}, u32[]{:S(2)}, u32[]{:S(2)}) %collective-permute-start) | collective-permute-done | bytes 1638432 | tf_op jit(solution)/shard_map/while/body/eval_jaxpr/ppermute | solution.py:10
  164.9 7.6 %collective-permute-done = bf16[5,10,128,128]{3,2,0,1:T(8,128)(2,1)S(1)} collective-permute-done((bf16[5,10,128,128]{3,2,0,1:T(8,128)(2,1)S(1)}, bf16[5,10,128,128]{3,2,0,1:T(8,128)(2,1)S(1)}, u32[]{:S(2)}, u32[]{:S(2)}) %collective-permute-start) | collective-permute-done | bytes 1638432 | tf_op jit(solution)/shard_map/while/body/eval_jaxpr/ppermute | solution.py:10
  172.6 6.1 %collective-permute-start = (bf16[5,10,128,128]{3,2,0,1:T(8,128)(2,1)S(1)}, bf16[5,10,128,128]{3,2,0,1:T(8,128)(2,1)S(1)}, u32[]{:S(2)}, u32[]{:S(2)}) collective-permute-start(bf16[5,10,128,128]{3,2,0,1:T(8,128)(2,1)S(1)} %copy.82), channel_id=1, source_target_pairs={{0,8},{8,16},{16,24},{24,32},{32,40},{40,48},{48,56},{56,64},{64,7... | collective-permute-start | bytes 4915208 | tf_op jit(solution)/shard_map/while/body/eval_jaxpr/ppermute | solution.py:10
  186.6 6.7 %collective-permute-done = bf16[5,10,128,128]{3,2,0,1:T(8,128)(2,1)S(1)} collective-permute-done((bf16[5,10,128,128]{3,2,0,1:T(8,128)(2,1)S(1)}, bf16[5,10,128,128]{3,2,0,1:T(8,128)(2,1)S(1)}, u32[]{:S(2)}, u32[]{:S(2)}) %collective-permute-start) | collective-permute-done | bytes 1638432 | tf_op jit(solution)/shard_map/while/body/eval_jaxpr/ppermute | solution.py:10
  193.3 7.0 %collective-permute-start = (bf16[5,10,128,128]{3,2,0,1:T(8,128)(2,1)S(1)}, bf16[5,10,128,128]{3,2,0,1:T(8,128)(2,1)S(1)}, u32[]{:S(2)}, u32[]{:S(2)}) collective-permute-start(bf16[5,10,128,128]{3,2,0,1:T(8,128)(2,1)S(1)} %copy.82), channel_id=1, source_target_pairs={{0,8},{8,16},{16,24},{24,32},{32,40},{40,48},{48,56},{56,64},{64,7... | collective-permute-start | bytes 4915208 | tf_op jit(solution)/shard_map/while/body/eval_jaxpr/ppermute | solution.py:10
  208.2 5.8 %collective-permute-done = bf16[5,10,128,128]{3,2,0,1:T(8,128)(2,1)S(1)} collective-permute-done((bf16[5,10,128,128]{3,2,0,1:T(8,128)(2,1)S(1)}, bf16[5,10,128,128]{3,2,0,1:T(8,128)(2,1)S(1)}, u32[]{:S(2)}, u32[]{:S(2)}) %collective-permute-start) | collective-permute-done | bytes 1638432 | tf_op jit(solution)/shard_map/while/body/eval_jaxpr/ppermute | solution.py:10
  214.0 7.9 %collective-permute-start = (bf16[5,10,128,128]{3,2,0,1:T(8,128)(2,1)S(1)}, bf16[5,10,128,128]{3,2,0,1:T(8,128)(2,1)S(1)}, u32[]{:S(2)}, u32[]{:S(2)}) collective-permute-start(bf16[5,10,128,128]{3,2,0,1:T(8,128)(2,1)S(1)} %copy.82), channel_id=1, source_target_pairs={{0,8},{8,16},{16,24},{24,32},{32,40},{40,48},{48,56},{56,64},{64,7... | collective-permute-start | bytes 4915208 | tf_op jit(solution)/shard_map/while/body/eval_jaxpr/ppermute | solution.py:10
  229.8 5.8 %collective-permute-done = bf16[5,10,128,128]{3,2,0,1:T(8,128)(2,1)S(1)} collective-permute-done((bf16[5,10,128,128]{3,2,0,1:T(8,128)(2,1)S(1)}, bf16[5,10,128,128]{3,2,0,1:T(8,128)(2,1)S(1)}, u32[]{:S(2)}, u32[]{:S(2)}) %collective-permute-start) | collective-permute-done | bytes 1638432 | tf_op jit(solution)/shard_map/while/body/eval_jaxpr/ppermute | solution.py:10
  235.7 7.9 %collective-permute-start = (bf16[5,10,128,128]{3,2,0,1:T(8,128)(2,1)S(1)}, bf16[5,10,128,128]{3,2,0,1:T(8,128)(2,1)S(1)}, u32[]{:S(2)}, u32[]{:S(2)}) collective-permute-start(bf16[5,10,128,128]{3,2,0,1:T(8,128)(2,1)S(1)} %copy.82), channel_id=1, source_target_pairs={{0,8},{8,16},{16,24},{24,32},{32,40},{40,48},{48,56},{56,64},{64,7... | collective-permute-start | bytes 4915208 | tf_op jit(solution)/shard_map/while/body/eval_jaxpr/ppermute | solution.py:10
  246.2 5.2 %bitcast_add_fusion.4 = f32[5,10,128,128]{3,2,0,1:T(8,128)} fusion(f32[5,10,128,128]{3,2,0,1:T(8,128)} %get-tuple-element.325, bf16[5,10,5]{2,0,1:T(8,128)(2,1)S(1)} %copy.76, bf16[5,5,128,128]{3,2,1,0:T(8,128)(2,1)S(1)} %constant_dynamic-slice_fusion.3, bf16[5,10,128,128]{3,2,0,1:T(8,128)(2,1)S(1)} %copy.82, pred[]{:T(512)S(6)} %compare.5), kind=kOutput, calls=%fused_computation.5.clone.1 | convolution fusion | flops 1054310400 | bytes 9011701 | tf_op jit(solution)/shard_map/while/body/eval_jaxpr/ijkac,kjcb->ijab/dot_general | solution.py:33
  251.4 7.0 %collective-permute-done = bf16[5,10,128,128]{3,2,0,1:T(8,128)(2,1)S(1)} collective-permute-done((bf16[5,10,128,128]{3,2,0,1:T(8,128)(2,1)S(1)}, bf16[5,10,128,128]{3,2,0,1:T(8,128)(2,1)S(1)}, u32[]{:S(2)}, u32[]{:S(2)}) %collective-permute-start) | collective-permute-done | bytes 1638432 | tf_op jit(solution)/shard_map/while/body/eval_jaxpr/ppermute | solution.py:10
  258.5 6.7 %collective-permute-start = (bf16[5,10,128,128]{3,2,0,1:T(8,128)(2,1)S(1)}, bf16[5,10,128,128]{3,2,0,1:T(8,128)(2,1)S(1)}, u32[]{:S(2)}, u32[]{:S(2)}) collective-permute-start(bf16[5,10,128,128]{3,2,0,1:T(8,128)(2,1)S(1)} %copy.82), channel_id=1, source_target_pairs={{0,8},{8,16},{16,24},{24,32},{32,40},{40,48},{48,56},{56,64},{64,7... | collective-permute-start | bytes 4915208 | tf_op jit(solution)/shard_map/while/body/eval_jaxpr/ppermute | solution.py:10
  267.8 5.2 %bitcast_add_fusion.4 = f32[5,10,128,128]{3,2,0,1:T(8,128)} fusion(f32[5,10,128,128]{3,2,0,1:T(8,128)} %get-tuple-element.325, bf16[5,10,5]{2,0,1:T(8,128)(2,1)S(1)} %copy.76, bf16[5,5,128,128]{3,2,1,0:T(8,128)(2,1)S(1)} %constant_dynamic-slice_fusion.3, bf16[5,10,128,128]{3,2,0,1:T(8,128)(2,1)S(1)} %copy.82, pred[]{:T(512)S(6)} %compare.5), kind=kOutput, calls=%fused_computation.5.clone.1 | convolution fusion | flops 1054310400 | bytes 9011701 | tf_op jit(solution)/shard_map/while/body/eval_jaxpr/ijkac,kjcb->ijab/dot_general | solution.py:33
  273.1 8.2 %collective-permute-done = bf16[5,10,128,128]{3,2,0,1:T(8,128)(2,1)S(1)} collective-permute-done((bf16[5,10,128,128]{3,2,0,1:T(8,128)(2,1)S(1)}, bf16[5,10,128,128]{3,2,0,1:T(8,128)(2,1)S(1)}, u32[]{:S(2)}, u32[]{:S(2)}) %collective-permute-start) | collective-permute-done | bytes 1638432 | tf_op jit(solution)/shard_map/while/body/eval_jaxpr/ppermute | solution.py:10
  281.3 5.5 %collective-permute-start = (bf16[5,10,128,128]{3,2,0,1:T(8,128)(2,1)S(1)}, bf16[5,10,128,128]{3,2,0,1:T(8,128)(2,1)S(1)}, u32[]{:S(2)}, u32[]{:S(2)}) collective-permute-start(bf16[5,10,128,128]{3,2,0,1:T(8,128)(2,1)S(1)} %copy.82), channel_id=1, source_target_pairs={{0,8},{8,16},{16,24},{24,32},{32,40},{40,48},{48,56},{56,64},{64,7... | collective-permute-start | bytes 4915208 | tf_op jit(solution)/shard_map/while/body/eval_jaxpr/ppermute | solution.py:10
  294.7 9.4 %collective-permute-done = bf16[5,10,128,128]{3,2,0,1:T(8,128)(2,1)S(1)} collective-permute-done((bf16[5,10,128,128]{3,2,0,1:T(8,128)(2,1)S(1)}, bf16[5,10,128,128]{3,2,0,1:T(8,128)(2,1)S(1)}, u32[]{:S(2)}, u32[]{:S(2)}) %collective-permute-start) | collective-permute-done | bytes 1638432 | tf_op jit(solution)/shard_map/while/body/eval_jaxpr/ppermute | solution.py:10
  316.3 10.6 %collective-permute-done = bf16[5,10,128,128]{3,2,0,1:T(8,128)(2,1)S(1)} collective-permute-done((bf16[5,10,128,128]{3,2,0,1:T(8,128)(2,1)S(1)}, bf16[5,10,128,128]{3,2,0,1:T(8,128)(2,1)S(1)}, u32[]{:S(2)}, u32[]{:S(2)}) %collective-permute-start) | collective-permute-done | bytes 1638432 | tf_op jit(solution)/shard_map/while/body/eval_jaxpr/ppermute | solution.py:10
  331.5 6.4 %bitcast_add_fusion.2 = f32[5,10,128,128]{2,3,0,1:T(8,128)} fusion(f32[5,10,128,128]{2,3,0,1:T(8,128)} %copy.56, bf16[5,10,5]{2,0,1:T(8,128)(2,1)S(1)} %copy.54, bf16[5,5,128,128]{3,2,1,0:T(8,128)(2,1)S(1)} %copy-done.2, bf16[5,10,128,128]{3,2,0,1:T(8,128)(2,1)S(1)} %get-tuple-element.184), kind=kOutput, calls=%fused_computation.16 | convolution fusion | flops 1065779200 | bytes 9011700 | tf_op jit(solution)/shard_map/ijkac,kjcb->ijab/dot_general | solution.py:33
  337.9 5.5 %copy.57 = f32[5,10,128,128]{3,0,1,2:T(8,128)} copy(f32[5,10,128,128]{2,3,0,1:T(8,128)} %bitcast_add_fusion.2) | data formatting | bytes 6553600 | tf_op jit(solution)/shard_map/add | solution.py:33
  343.5 64.2 %all_to_all.54 = f32[5,10,128,128]{3,0,1,2:T(8,128)S(1)} all-to-all(f32[5,10,128,128]{3,0,1,2:T(8,128)} %copy.57), channel_id=1, replica_groups=mesh['row'=16,'col'=8] {'col'}, dimensions={2} | all-to-all | bytes 6553600 | tf_op jit(solution)/shard_map/all_to_all | solution.py:45
  409.0 49.5 %all_to_all.55 = f32[5,80,16,128]{3,2,0,1:T(8,128)S(1)} all-to-all(f32[5,80,16,128]{3,2,0,1:T(8,128)S(1)} %copy.60), channel_id=1, replica_groups=mesh['row'=16,'col'=8] {'row'}, dimensions={1} | all-to-all | bytes 6553600 | tf_op jit(solution)/shard_map/all_to_all | solution.py:47
  458.7 44.1 %all_to_all.56 = f32[80,5,16,128]{3,2,1,0:T(8,128)S(1)} all-to-all(f32[80,5,16,128]{3,2,1,0:T(8,128)S(1)} %bitcast.41), channel_id=1, replica_groups=mesh['row'=16,'col'=8] {'col'}, dimensions={0} | all-to-all | bytes 6553600 | tf_op jit(solution)/shard_map/all_to_all | solution.py:46
  (163 shorter events, 135.2 us)
Async XLA Ops:
  0.0 6.7 %copy-start.3 = (s32[5,10]{1,0:T(8,128)S(1)}, s32[5,10]{1,0:T(8,128)}, u32[]{:S(2)}) copy-start(s32[5,10]{1,0:T(8,128)} %param.9) | copy-start | bytes 604
  0.0 6.7 %copy-start.1 = (s32[5,10,48]{2,1,0:T(8,128)S(1)}, s32[5,10,48]{2,1,0:T(8,128)}, u32[]{:S(2)}) copy-start(s32[5,10,48]{2,1,0:T(8,128)} %param.8) | copy-start | bytes 28804
  6.8 20.6 %collective-permute-start = (bf16[5,10,128,128]{3,2,0,1:T(8,128)(2,1)S(1)}, bf16[5,10,128,128]{3,2,0,1:T(8,128)(2,1)S(1)}, u32[]{:S(2)}, u32[]{:S(2)}) collective-permute-start(bf16[5,10,128,128]{3,2,0,1:T(8,128)(2,1)S(1)} %copy.82), channel_id=1, source_target_pairs={{0,8},{8,16},{16,24},{24,32},{32,40},{40,48},{48,56},{56,64},{64,7... | collective-permute-start | bytes 4915208 | tf_op jit(solution)/shard_map/while/body/eval_jaxpr/ppermute | solution.py:10
  27.5 20.6 %collective-permute-start = (bf16[5,10,128,128]{3,2,0,1:T(8,128)(2,1)S(1)}, bf16[5,10,128,128]{3,2,0,1:T(8,128)(2,1)S(1)}, u32[]{:S(2)}, u32[]{:S(2)}) collective-permute-start(bf16[5,10,128,128]{3,2,0,1:T(8,128)(2,1)S(1)} %copy.82), channel_id=1, source_target_pairs={{0,8},{8,16},{16,24},{24,32},{32,40},{40,48},{48,56},{56,64},{64,7... | collective-permute-start | bytes 4915208 | tf_op jit(solution)/shard_map/while/body/eval_jaxpr/ppermute | solution.py:10
  48.2 20.6 %collective-permute-start = (bf16[5,10,128,128]{3,2,0,1:T(8,128)(2,1)S(1)}, bf16[5,10,128,128]{3,2,0,1:T(8,128)(2,1)S(1)}, u32[]{:S(2)}, u32[]{:S(2)}) collective-permute-start(bf16[5,10,128,128]{3,2,0,1:T(8,128)(2,1)S(1)} %copy.82), channel_id=1, source_target_pairs={{0,8},{8,16},{16,24},{24,32},{32,40},{40,48},{48,56},{56,64},{64,7... | collective-permute-start | bytes 4915208 | tf_op jit(solution)/shard_map/while/body/eval_jaxpr/ppermute | solution.py:10
  69.0 20.6 %collective-permute-start = (bf16[5,10,128,128]{3,2,0,1:T(8,128)(2,1)S(1)}, bf16[5,10,128,128]{3,2,0,1:T(8,128)(2,1)S(1)}, u32[]{:S(2)}, u32[]{:S(2)}) collective-permute-start(bf16[5,10,128,128]{3,2,0,1:T(8,128)(2,1)S(1)} %copy.82), channel_id=1, source_target_pairs={{0,8},{8,16},{16,24},{24,32},{32,40},{40,48},{48,56},{56,64},{64,7... | collective-permute-start | bytes 4915208 | tf_op jit(solution)/shard_map/while/body/eval_jaxpr/ppermute | solution.py:10
  89.7 20.6 %collective-permute-start = (bf16[5,10,128,128]{3,2,0,1:T(8,128)(2,1)S(1)}, bf16[5,10,128,128]{3,2,0,1:T(8,128)(2,1)S(1)}, u32[]{:S(2)}, u32[]{:S(2)}) collective-permute-start(bf16[5,10,128,128]{3,2,0,1:T(8,128)(2,1)S(1)} %copy.82), channel_id=1, source_target_pairs={{0,8},{8,16},{16,24},{24,32},{32,40},{40,48},{48,56},{56,64},{64,7... | collective-permute-start | bytes 4915208 | tf_op jit(solution)/shard_map/while/body/eval_jaxpr/ppermute | solution.py:10
  110.4 20.6 %collective-permute-start = (bf16[5,10,128,128]{3,2,0,1:T(8,128)(2,1)S(1)}, bf16[5,10,128,128]{3,2,0,1:T(8,128)(2,1)S(1)}, u32[]{:S(2)}, u32[]{:S(2)}) collective-permute-start(bf16[5,10,128,128]{3,2,0,1:T(8,128)(2,1)S(1)} %copy.82), channel_id=1, source_target_pairs={{0,8},{8,16},{16,24},{24,32},{32,40},{40,48},{48,56},{56,64},{64,7... | collective-permute-start | bytes 4915208 | tf_op jit(solution)/shard_map/while/body/eval_jaxpr/ppermute | solution.py:10
  131.1 20.6 %collective-permute-start = (bf16[5,10,128,128]{3,2,0,1:T(8,128)(2,1)S(1)}, bf16[5,10,128,128]{3,2,0,1:T(8,128)(2,1)S(1)}, u32[]{:S(2)}, u32[]{:S(2)}) collective-permute-start(bf16[5,10,128,128]{3,2,0,1:T(8,128)(2,1)S(1)} %copy.82), channel_id=1, source_target_pairs={{0,8},{8,16},{16,24},{24,32},{32,40},{40,48},{48,56},{56,64},{64,7... | collective-permute-start | bytes 4915208 | tf_op jit(solution)/shard_map/while/body/eval_jaxpr/ppermute | solution.py:10
  151.9 20.6 %collective-permute-start = (bf16[5,10,128,128]{3,2,0,1:T(8,128)(2,1)S(1)}, bf16[5,10,128,128]{3,2,0,1:T(8,128)(2,1)S(1)}, u32[]{:S(2)}, u32[]{:S(2)}) collective-permute-start(bf16[5,10,128,128]{3,2,0,1:T(8,128)(2,1)S(1)} %copy.82), channel_id=1, source_target_pairs={{0,8},{8,16},{16,24},{24,32},{32,40},{40,48},{48,56},{56,64},{64,7... | collective-permute-start | bytes 4915208 | tf_op jit(solution)/shard_map/while/body/eval_jaxpr/ppermute | solution.py:10
  172.6 20.6 %collective-permute-start = (bf16[5,10,128,128]{3,2,0,1:T(8,128)(2,1)S(1)}, bf16[5,10,128,128]{3,2,0,1:T(8,128)(2,1)S(1)}, u32[]{:S(2)}, u32[]{:S(2)}) collective-permute-start(bf16[5,10,128,128]{3,2,0,1:T(8,128)(2,1)S(1)} %copy.82), channel_id=1, source_target_pairs={{0,8},{8,16},{16,24},{24,32},{32,40},{40,48},{48,56},{56,64},{64,7... | collective-permute-start | bytes 4915208 | tf_op jit(solution)/shard_map/while/body/eval_jaxpr/ppermute | solution.py:10
  193.3 20.6 %collective-permute-start = (bf16[5,10,128,128]{3,2,0,1:T(8,128)(2,1)S(1)}, bf16[5,10,128,128]{3,2,0,1:T(8,128)(2,1)S(1)}, u32[]{:S(2)}, u32[]{:S(2)}) collective-permute-start(bf16[5,10,128,128]{3,2,0,1:T(8,128)(2,1)S(1)} %copy.82), channel_id=1, source_target_pairs={{0,8},{8,16},{16,24},{24,32},{32,40},{40,48},{48,56},{56,64},{64,7... | collective-permute-start | bytes 4915208 | tf_op jit(solution)/shard_map/while/body/eval_jaxpr/ppermute | solution.py:10
  214.0 21.5 %collective-permute-start = (bf16[5,10,128,128]{3,2,0,1:T(8,128)(2,1)S(1)}, bf16[5,10,128,128]{3,2,0,1:T(8,128)(2,1)S(1)}, u32[]{:S(2)}, u32[]{:S(2)}) collective-permute-start(bf16[5,10,128,128]{3,2,0,1:T(8,128)(2,1)S(1)} %copy.82), channel_id=1, source_target_pairs={{0,8},{8,16},{16,24},{24,32},{32,40},{40,48},{48,56},{56,64},{64,7... | collective-permute-start | bytes 4915208 | tf_op jit(solution)/shard_map/while/body/eval_jaxpr/ppermute | solution.py:10
  235.7 22.7 %collective-permute-start = (bf16[5,10,128,128]{3,2,0,1:T(8,128)(2,1)S(1)}, bf16[5,10,128,128]{3,2,0,1:T(8,128)(2,1)S(1)}, u32[]{:S(2)}, u32[]{:S(2)}) collective-permute-start(bf16[5,10,128,128]{3,2,0,1:T(8,128)(2,1)S(1)} %copy.82), channel_id=1, source_target_pairs={{0,8},{8,16},{16,24},{24,32},{32,40},{40,48},{48,56},{56,64},{64,7... | collective-permute-start | bytes 4915208 | tf_op jit(solution)/shard_map/while/body/eval_jaxpr/ppermute | solution.py:10
  258.5 22.7 %collective-permute-start = (bf16[5,10,128,128]{3,2,0,1:T(8,128)(2,1)S(1)}, bf16[5,10,128,128]{3,2,0,1:T(8,128)(2,1)S(1)}, u32[]{:S(2)}, u32[]{:S(2)}) collective-permute-start(bf16[5,10,128,128]{3,2,0,1:T(8,128)(2,1)S(1)} %copy.82), channel_id=1, source_target_pairs={{0,8},{8,16},{16,24},{24,32},{32,40},{40,48},{48,56},{56,64},{64,7... | collective-permute-start | bytes 4915208 | tf_op jit(solution)/shard_map/while/body/eval_jaxpr/ppermute | solution.py:10
  281.3 22.7 %collective-permute-start = (bf16[5,10,128,128]{3,2,0,1:T(8,128)(2,1)S(1)}, bf16[5,10,128,128]{3,2,0,1:T(8,128)(2,1)S(1)}, u32[]{:S(2)}, u32[]{:S(2)}) collective-permute-start(bf16[5,10,128,128]{3,2,0,1:T(8,128)(2,1)S(1)} %copy.82), channel_id=1, source_target_pairs={{0,8},{8,16},{16,24},{24,32},{32,40},{40,48},{48,56},{56,64},{64,7... | collective-permute-start | bytes 4915208 | tf_op jit(solution)/shard_map/while/body/eval_jaxpr/ppermute | solution.py:10
  304.2 22.7 %collective-permute-start = (bf16[5,10,128,128]{3,2,0,1:T(8,128)(2,1)S(1)}, bf16[5,10,128,128]{3,2,0,1:T(8,128)(2,1)S(1)}, u32[]{:S(2)}, u32[]{:S(2)}) collective-permute-start(bf16[5,10,128,128]{3,2,0,1:T(8,128)(2,1)S(1)} %copy.82), channel_id=1, source_target_pairs={{0,8},{8,16},{16,24},{24,32},{32,40},{40,48},{48,56},{56,64},{64,7... | collective-permute-start | bytes 4915208 | tf_op jit(solution)/shard_map/while/body/eval_jaxpr/ppermute | solution.py:10
  326.9 4.6 copy-start.2
  502.8 1.9 copy-start
where the time goes:
time: 518 us; the launch traced here: 512 us
  blocking collectives  158 us (31%)
  waiting for transfers between devices  139 us (27%)
  matrix products  83.6 us (16%)
  starting transfers between devices  63 us (12%)
  local copies, waits for them, and re-layouts  46.4 us (9%)
  other arithmetic  21.3 us (4%)
    ppermute x15, waiting for transfers between devices, shifted(): return lax.ppermute(value, axis, pairs)  139 us
    dot_general x16, matrix products, contribute(): jnp.einsum('ijkac,kjcb->ijab', masked, integral_block, preferred_element_...  83.6 us
    all_to_all x1, blocking collectives, on_device(): lax.all_to_all(contracted, 'col', split_axis=2, concat_axis=1, tiled=True)  64.2 us
    ppermute x15, starting transfers between devices, shifted(): return lax.ppermute(value, axis, pairs)  63 us
    all_to_all x1, blocking collectives, on_device(): lax.all_to_all(section_one, 'row', split_axis=1, concat_axis=0, tiled=True)  49.5 us
    all_to_all x1, blocking collectives, on_device(): lax.all_to_all(lax.all_to_all(section_one, 'row', split_axis=1, concat_ax...  44.1 us
    dynamic_slice x16, local copies, waits for them, and re-layouts, contribute(): amp_piece = lax.dynamic_slice_in_dim(amplitudes, first_k, kblock, 1)  20.5 us
    reduce_or x16, other arithmetic, contribute(): alive_mask = jnp.any(matches, axis=2).astype(jnp.bfloat16)  16.9 us
  transfers between devices with their start and end apart: 15, of which 15 were waited for; matrix products, arithmetic and copies ran while one was open for 23% of the time, Pallas kernels for 0%

commit v1 on v0

v1 whole, which is shorter than its diff:
```python
import functools

import jax
import jax.numpy as jnp
from jax import lax
from jax.experimental import pallas as pl
from jax.experimental.pallas import tpu as pltpu
from jax.sharding import PartitionSpec as P

MESH = pl.DeviceIdType.MESH
TILE = 128
O = 80
HALF = 5
CHIP = 10
GROUPS = ((0, 1), (2, 3), (4,))
Y, BACK, FRONT, FAR, BACK_Y, FRONT_Y, FAR_Y = range(7)


def kernel(
    amp, integ, mask, direct, mirror,
    tv, wv, cyc, cyct, mv, ms,
    own_sem, pair_send, pair_recv, t_own, t_send, t_recv, m_sem,
    g_send, g_recv, d_own, d_send, d_recv, x_send, x_recv,
):
    row, col = lax.axis_index("row"), lax.axis_index("col")
    z, y, c = row // 4, (row // 2) % 2, row % 2
    chip = row // 2
    other = 1 - c
    sibling = (row + 1 - 2 * c, col)
    y_dev = (row + 2 - 4 * y, col)
    up = (lax.rem(row + 4, 16), col)
    down = (lax.rem(row + 12, 16), col)
    partner = (2 * col + c, chip)
    off_diagonal = chip != col

    def block(dz, dy):
        return lax.rem(z + dz + 4, 4) * 2 + (y if dy == 0 else 1 - y)

    barrier = pltpu.get_barrier_semaphore()
    for device in (sibling, y_dev, up, down):
        pl.semaphore_signal(barrier, inc=1, device_id=device, device_id_type=MESH)

    @pl.when(off_diagonal)
    def _():
        pl.semaphore_signal(barrier, inc=1, device_id=partner, device_id_type=MESH)
        pl.semaphore_wait(barrier, 5)

    @pl.when(jnp.logical_not(off_diagonal))
    def _():
        pl.semaphore_wait(barrier, 4)

    def remote(src, dst, send, recv, device):
        return pltpu.make_async_remote_copy(
            src_ref=src, dst_ref=dst, send_sem=send, recv_sem=recv, device_id=device, device_id_type=MESH
        )

    mine = pl.ds(chip * CHIP + c * HALF, HALF)
    theirs = pl.ds(chip * CHIP + other * HALF, HALF)
    own_w = [pltpu.make_async_copy(integ.at[:, c * HALF + j], wv.at[j, mine], own_sem.at[j]) for j in range(HALF)]
    pair_w = [
        remote(integ.at[:, other * HALF + j], wv.at[j, mine], pair_send.at[j], pair_recv.at[j], sibling)
        for j in range(HALF)
    ]
    for j in range(HALF):
        own_w[j].start()
        pair_w[j].start()

    mask_pair = remote(mask.at[other], mv, m_sem.at[0], m_sem.at[1], sibling)
    mask_pair.start()
    mask_own = pltpu.make_async_copy(mask.at[c], ms.at[c], m_sem.at[2])
    mask_own.start()

    def piece(kind, j, dz, dy):
        part = c if kind == 0 else other
        view = pl.ds(block(dz, dy) * CHIP + part * HALF, HALF)
        return wv.at[j, view]

    sends = []

    def send(kind, j, dz, dy, name, device):
        ref = piece(kind, j, dz, dy)
        slot = (j * 2 + kind) * 7 + name
        copy = remote(ref, ref, g_send.at[slot], g_recv.at[slot], device)
        copy.start()
        sends.append(copy)

    def arrived(kind, j, name):
        far = 1 if (kind + j) % 2 == 0 else -1
        dz, dy = {
            Y: (0, 1), BACK: (-far, 0), FRONT: (far, 0), FAR: (2, 0),
            BACK_Y: (-far, 1), FRONT_Y: (far, 1), FAR_Y: (2, 1),
        }[name]
        ref = piece(kind, j, dz, dy)
        slot = (j * 2 + kind) * 7 + name
        remote(ref, ref, g_send.at[slot], g_recv.at[slot], y_dev).wait_recv()

    def ahead(kind, j):
        plus = (kind + j) % 2 == 0
        return (up, down, 1) if plus else (down, up, -1)

    def stage0(j):
        for kind in range(2):
            front, back, far = ahead(kind, j)
            if kind == 0:
                own_w[j].wait()
            else:
                pair_w[j].wait_recv()
            send(kind, j, 0, 0, BACK, front)
            send(kind, j, 0, 0, FRONT, back)
            send(kind, j, 0, 0, Y, y_dev)

    def stage1(j):
        front, back, far = ahead(0, j)
        arrived(0, j, Y)
        send(0, j, 0, 1, BACK_Y, front)
        send(0, j, 0, 1, FRONT_Y, back)
        arrived(0, j, BACK)
        send(0, j, -far, 0, FAR, front)
        front, back, far = ahead(1, j)
        arrived(1, j, BACK)
        send(1, j, -far, 0, FAR, front)
        send(1, j, -far, 0, BACK_Y, y_dev)
        arrived(1, j, FRONT)
        send(1, j, far, 0, FRONT_Y, y_dev)

    def stage2(j):
        front, back, far = ahead(0, j)
        arrived(0, j, BACK_Y)
        send(0, j, -far, 1, FAR_Y, front)
        arrived(1, j, FAR)
        send(1, j, 2, 0, FAR_Y, y_dev)

    def near(j):
        arrived(0, j, FRONT)
        arrived(1, j, Y)

    def rest(j):
        for name in (FRONT_Y, FAR, FAR_Y):
            arrived(0, j, name)
        for name in (BACK_Y, FRONT_Y, FAR_Y):
            arrived(1, j, name)

    def contract(js, late):
        places = ((1, 1), (-1, 1), (2, 0), (2, 1)) if late else ((0, 0), (0, 1), (1, 0), (-1, 0))
        starts = [block(dz, dy) * CHIP for dz, dy in places]
        labels = [start + k for start in starts for k in range(CHIP)]

        def one(i, carry):
            left = jnp.concatenate([tv[i, k] for k in labels], axis=1)
            right = []
            for j in js:
                right.append(
                    jnp.concatenate(
                        [
                            wv[j, k] * jnp.full((TILE, TILE), ms[i // HALF, lax.rem(i, HALF) * HALF + j, k], jnp.float32).astype(jnp.bfloat16)
                            for k in labels
                        ],
                        axis=0,
                    )
                )
            right = right[0] if len(js) == 1 else jnp.concatenate(right, axis=1)
            out = jnp.dot(left, right, preferred_element_type=jnp.float32)
            for n, j in enumerate(js):
                tile = out[:, n * TILE : (n + 1) * TILE]
                if late:
                    tile = tile + cyc[j, i]
                    cyct[j, i] = tile.T
                cyc[j, i] = tile
            return carry

        lax.fori_loop(0, CHIP, one, 0)

    finals = []

    def hand_out(j):
        own = pltpu.make_async_copy(cyc.at[j, pl.ds(c * HALF, HALF)], direct.at[:, c * HALF + j], d_own.at[j])
        own.start()
        pair = remote(
            cyc.at[j, pl.ds(other * HALF, HALF)], direct.at[:, c * HALF + j], d_send.at[j], d_recv.at[j], sibling
        )
        pair.start()

        @pl.when(off_diagonal)
        def _():
            remote(cyct.at[j], mirror.at[j], x_send.at[j], x_recv.at[j], partner).start()

        @pl.when(jnp.logical_not(off_diagonal))
        def _():
            pltpu.make_async_copy(cyct.at[j], mirror.at[j], x_send.at[j]).start()

        finals.append((own, pair))

    t_local = [pltpu.make_async_copy(amp.at[i], tv.at[c * HALF + i], t_own.at[i]) for i in range(HALF)]
    t_pair = [remote(amp.at[i], tv.at[c * HALF + i], t_send.at[i], t_recv.at[i], sibling) for i in range(HALF)]

    stage0(0)
    for i in range(HALF):
        t_local[i].start()
        t_pair[i].start()
    stage0(1)
    stage1(0)
    stage0(2)
    stage1(1)
    stage2(0)
    stage0(3)
    stage1(2)
    stage2(1)
    near(0)
    near(1)
    mask_pair.wait()
    mask_own.wait()
    second = pltpu.make_async_copy(mv, ms.at[other], m_sem.at[2])
    second.start()
    second.wait()
    for i in range(HALF):
        t_local[i].wait()
        t_pair[i].wait()
    contract(GROUPS[0], False)
    stage0(4)
    stage1(3)
    stage2(2)
    rest(0)
    rest(1)
    contract(GROUPS[0], True)
    hand_out(0)
    hand_out(1)
    stage1(4)
    stage2(3)
    near(2)
    near(3)
    contract(GROUPS[1], False)
    stage2(4)
    rest(2)
    rest(3)
    contract(GROUPS[1], True)
    hand_out(2)
    hand_out(3)
    near(4)
    contract(GROUPS[2], False)
    rest(4)
    contract(GROUPS[2], True)
    hand_out(4)

    for copy in sends:
        copy.wait_send()
    for copy in pair_w:
        copy.wait_send()
    for own, pair in finals:
        own.wait()
        pair.wait()
    for j in range(HALF):
        @pl.when(off_diagonal)
        def _():
            remote(cyct.at[j], mirror.at[j], x_send.at[j], x_recv.at[j], partner).wait()

        @pl.when(jnp.logical_not(off_diagonal))
        def _():
            pltpu.make_async_copy(cyct.at[j], mirror.at[j], x_send.at[j]).wait()


def on_device(amplitudes, integrals, pair_lists, pair_counts):
    rows_here, cols_here, slots = pair_lists.shape
    in_count = jnp.arange(slots, dtype=jnp.int32)[None, None, :] < pair_counts[:, :, None]
    labels = jnp.arange(TILE, dtype=jnp.int32)
    live = jnp.any(
        (pair_lists[:, :, :, None] == labels[None, None, None, :]) & in_count[:, :, :, None], axis=2
    ).astype(jnp.float32)
    mask = live.reshape(rows_here, 2, HALF, TILE).transpose(1, 0, 2, 3).reshape(2, HALF * HALF, TILE)
    mask = jnp.pad(mask, ((0, 0), (0, 32 - HALF * HALF), (0, 0)))
    bf, f32 = jnp.bfloat16, jnp.float32
    dma = pltpu.SemaphoreType.DMA
    tiles = jax.ShapeDtypeStruct((HALF, CHIP, TILE, TILE), f32)
    anywhere = pl.BlockSpec(memory_space=pl.ANY)
    direct, mirror = pl.pallas_call(
        kernel,
        out_shape=(tiles, tiles),
        in_specs=[anywhere] * 3,
        out_specs=(anywhere, anywhere),
        scratch_shapes=[
            pltpu.VMEM((CHIP, O, TILE, TILE), bf),
            pltpu.VMEM((HALF, O, TILE, TILE), bf),
            pltpu.VMEM((HALF, CHIP, TILE, TILE), f32),
            pltpu.VMEM((HALF, CHIP, TILE, TILE), f32),
            pltpu.VMEM((32, TILE), f32),
            pltpu.SMEM((2, 32, TILE), f32),
            dma((HALF,)), dma((HALF,)), dma((HALF,)), dma((HALF,)), dma((HALF,)), dma((HALF,)), dma((3,)),
            dma((70,)), dma((70,)), dma((HALF,)), dma((HALF,)), dma((HALF,)), dma((HALF,)), dma((HALF,)),
        ],
        compiler_params=pltpu.CompilerParams(
            collective_id=0, has_side_effects=True, vmem_limit_bytes=60 * 1024 * 1024
        ),
        cost_estimate=pl.CostEstimate(flops=17_000_000_000, bytes_accessed=60_000_000, transcendentals=0),
    )(amplitudes, integrals, mask)
    return direct + mirror


def solution(mesh):
    placed = (
        P("row", None, None, None),
        P("row", "col", None, None),
        P("row", "col", None),
        P("row", "col"),
    )
    return jax.shard_map(
        on_device,
        mesh=mesh,
        in_specs=placed,
        out_specs=P("row", "col", None, None),
        check_vma=False,
    )
```

time: 518 us -> 362 us (0.70)
  the two profiles are of different devices: /device:TPU:28 before, /device:TPU:8 now
where the time goes in v1:
time: 362 us
  Pallas kernels  353 us (98%)
  other arithmetic  8.71 us (2%)
    pallas_call x1, Pallas kernels, on_device(): pl.pallas_call(kernel, out_shape=(tiles, tiles), in_specs=[anywhere] * 3,...  353 us

profile of v1, /device:TPU:8, one launch (start us, length us, event | category | flops | bytes accessed | tf_op | source)
XLA Modules:
  0.0 361.7 jit_solution(5301258121925275947)
XLA Ops:
  0.0 0.8 iota_compare_fusion.1
  0.8 2.0 fusion.1
  2.8 0.6 pad_convert_fusion.mask
  3.4 352.9 %shard_map.46 = (f32[5,10,128,128]{3,2,1,0:T(8,128)}, f32[5,10,128,128]{3,2,1,0:T(8,128)}) custom-call(bf16[5,80,128,128]{3,2,1,0:T(8,128)(2,1)} %amp.1, bf16[5,10,128,128]{3,2,1,0:T(8,128)(2,1)} %integ.1, f32[2,32,128]{2,1,0:T(8,128)} %pad_convert_fusion.mask), custom_call_target="tpu_custom_call" | custom-call | flops 16999999488 | bytes 60000000 | tf_op jit(solution)/shard_map/pallas_call | solution.py:274
  356.4 5.4 %add.3 = f32[5,10,128,128]{3,2,1,0:T(8,128)} add(f32[5,10,128,128]{3,2,1,0:T(8,128)} %get-tuple-element.7, f32[5,10,128,128]{3,2,1,0:T(8,128)} %get-tuple-element.8) | non-fusion elementwise | flops 819200 | bytes 9830400 | tf_op jit(solution)/shard_map/add | solution.py:294
  (3 shorter events, 0.0 us)

commit v2 on v1

--- a/solution.py
+++ b/solution.py
@@ -13,14 +13,17 @@
 HALF = 5
 CHIP = 10
 GROUPS = ((0, 1), (2, 3), (4,))
+PACK = HALF * TILE + 16
+TOP = 2.0**15
 Y, BACK, FRONT, FAR, BACK_Y, FRONT_Y, FAR_Y = range(7)
 
 
 def kernel(
-    amp, integ, mask, direct, mirror,
-    tv, wv, cyc, cyct, mv, ms,
+    amp, integ, lists, counts, direct, mirror,
+    tv, wv, cyc, code, via_y, via_z, mine_v, mv, ms,
     own_sem, pair_send, pair_recv, t_own, t_send, t_recv, m_sem,
-    g_send, g_recv, d_own, d_send, d_recv, x_send, x_recv,
+    g_send, g_recv, d_own, d_send, d_recv,
+    y_send, y_recv, z_send, z_recv, a_send, a_recv, b_send, b_recv, c_send,
 ):
     row, col = lax.axis_index("row"), lax.axis_index("col")
     z, y, c = row // 4, (row // 2) % 2, row % 2
@@ -30,24 +33,54 @@
     y_dev = (row + 2 - 4 * y, col)
     up = (lax.rem(row + 4, 16), col)
     down = (lax.rem(row + 12, 16), col)
-    partner = (2 * col + c, chip)
-    off_diagonal = chip != col
+    x, y_hi = col // 2, col % 2
+    delta = lax.rem(z - x + 4, 4)
+
+    def at(px, lo, hi, pz):
+        return (pz * 4 + lo * 2 + c, px * 2 + hi)
+
+    crossing = y != y_hi
+    diagonal = delta == 0
+    turned = jnp.logical_not(diagonal)
+    stays = jnp.logical_and(diagonal, jnp.logical_not(crossing))
+    swapped = at(x, y_hi, y, z)
+    flipped = at(z, y, y_hi, x)
+    corner = at(x, y, y_hi, x)
+    opposite = at(x, y, y_hi, lax.rem(z + 2, 4))
 
     def block(dz, dy):
         return lax.rem(z + dz + 4, 4) * 2 + (y if dy == 0 else 1 - y)
 
     barrier = pltpu.get_barrier_semaphore()
+
+    def greet(device):
+        pl.semaphore_signal(barrier, inc=1, device_id=device, device_id_type=MESH)
+
     for device in (sibling, y_dev, up, down):
-        pl.semaphore_signal(barrier, inc=1, device_id=device, device_id_type=MESH)
-
-    @pl.when(off_diagonal)
+        greet(device)
+
+    @pl.when(crossing)
     def _():
-        pl.semaphore_signal(barrier, inc=1, device_id=partner, device_id_type=MESH)
-        pl.semaphore_wait(barrier, 5)
-
-    @pl.when(jnp.logical_not(off_diagonal))
+        greet(swapped)
+
+    @pl.when(turned)
     def _():
-        pl.semaphore_wait(barrier, 4)
+        greet(flipped)
+        greet(at(z, y_hi, y, z))
+
+    @pl.when(lax.rem(delta, 2) == 0)
+    def _():
+        greet(opposite)
+
+    @pl.when(diagonal)
+    def _():
+        for step in range(1, 4):
+            greet(at(lax.rem(x + step, 4), y_hi, y, z))
+
+    peers = (
+        4 + jnp.where(crossing, 1, 0) + jnp.where(turned, 2, 3) + jnp.where(lax.rem(delta, 2) == 0, 1, 0)
+    )
+    pl.semaphore_wait(barrier, peers)
 
     def remote(src, dst, send, recv, device):
         return pltpu.make_async_remote_copy(
@@ -65,10 +98,24 @@
         own_w[j].start()
         pair_w[j].start()
 
-    mask_pair = remote(mask.at[other], mv, m_sem.at[0], m_sem.at[1], sibling)
-    mask_pair.start()
-    mask_own = pltpu.make_async_copy(mask.at[c], ms.at[c], m_sem.at[2])
-    mask_own.start()
+    mask_pair = remote(mine_v.at[other], mv, m_sem.at[0], m_sem.at[1], sibling)
+    mask_own = pltpu.make_async_copy(mine_v.at[c], ms.at[c], m_sem.at[2])
+
+    def make_mask():
+        count_rows = counts[...]
+        slots = lists.shape[2]
+        eye = lax.broadcasted_iota(jnp.int32, (CHIP, CHIP), 0) == lax.broadcasted_iota(jnp.int32, (CHIP, CHIP), 1)
+        slot_ids = lax.broadcasted_iota(jnp.int32, (CHIP, slots), 1)
+        labels = lax.broadcasted_iota(jnp.int32, (CHIP, TILE), 1)
+        for i in range(HALF):
+            per_pair = jnp.broadcast_to(count_rows[i : i + 1], (CHIP, CHIP))
+            count = jnp.sum(jnp.where(eye, per_pair, 0), axis=1, keepdims=True)
+            kept = jnp.where(slot_ids < count, lists[i], -1)
+            live = jnp.zeros((CHIP, TILE), jnp.float32)
+            for s in range(slots):
+                live = jnp.where(kept[:, s : s + 1] == labels, 1.0, live)
+            for half in range(2):
+                mine_v[half, i * 8 : i * 8 + HALF] = live[half * HALF : (half + 1) * HALF]
 
     def piece(kind, j, dz, dy):
         part = c if kind == 0 else other
@@ -152,7 +199,7 @@
                 right.append(
                     jnp.concatenate(
                         [
-                            wv[j, k] * jnp.full((TILE, TILE), ms[i // HALF, lax.rem(i, HALF) * HALF + j, k], jnp.float32).astype(jnp.bfloat16)
+                            wv[j, k] * jnp.full((TILE, TILE), ms[i // HALF, lax.rem(i, HALF) * 8 + j, k], jnp.float32).astype(jnp.bfloat16)
                             for k in labels
                         ],
                         axis=0,
@@ -164,11 +211,113 @@
                 tile = out[:, n * TILE : (n + 1) * TILE]
                 if late:
                     tile = tile + cyc[j, i]
-                    cyct[j, i] = tile.T
+                    packed, scale = coded(tile.T)
+                    code[j, i // HALF, pl.ds(pl.multiple_of(lax.rem(i, HALF) * TILE, TILE), TILE)] = packed
+                    carry = carry[:n] + (jnp.where(rows == i + (i // HALF) * 3, scale, carry[n]),) + carry[n + 1 :]
                 cyc[j, i] = tile
             return carry
 
-        lax.fori_loop(0, CHIP, one, 0)
+        rows = lax.broadcasted_iota(jnp.int32, (16, TILE), 0)
+        scales = lax.fori_loop(0, CHIP, one, tuple(jnp.zeros((16, TILE), jnp.float32) for _ in js))
+        if late:
+            for n, j in enumerate(js):
+                for half in range(2):
+                    part = scales[n][half * 8 : half * 8 + 8]
+                    code[j, half, HALF * TILE : PACK] = jnp.concatenate([part, part], axis=0).astype(jnp.bfloat16)
+
+    def mirror_half(j, half):
+        return mirror.at[j, half]
+
+    def to_y(j):
+        return remote(code.at[j, 0], via_y.at[j], y_send.at[j], y_recv.at[j], swapped)
+
+    def to_corner(j):
+        slot = lax.rem(delta + 3, 4)
+        return remote(code.at[j, 1], via_z.at[slot, j], z_send.at[j], z_recv.at[slot, j], corner)
+
+    def straight(j, half, device):
+        send_sem, recv_sem = (a_send, a_recv) if half == 0 else (b_send, b_recv)
+        return remote(code.at[j, half], mirror_half(j, half), send_sem.at[j], recv_sem.at[j], device)
+
+    def local(j, half):
+        send_sem = a_send if half == 0 else b_send
+        return pltpu.make_async_copy(code.at[j, half], mirror_half(j, half), send_sem.at[j])
+
+    def second_a(j):
+        return remote(via_y.at[j], mirror_half(j, 0), a_send.at[j], a_recv.at[j], flipped)
+
+    def second_b(j, step):
+        device = at(lax.rem(x + step, 4), y_hi, y, z)
+        return remote(via_z.at[step - 1, j], mirror_half(j, 1), c_send.at[step - 1, j], b_recv.at[j], device)
+
+    both = jnp.logical_and(crossing, turned)
+    only_cross = jnp.logical_and(crossing, diagonal)
+    only_turn = jnp.logical_and(jnp.logical_not(crossing), turned)
+
+    def mirror_send(j):
+        @pl.when(both)
+        def _():
+            to_y(j).start()
+
+        @pl.when(only_turn)
+        def _():
+            straight(j, 0, flipped).start()
+
+        @pl.when(turned)
+        def _():
+            to_corner(j).start()
+
+        @pl.when(only_cross)
+        def _():
+            straight(j, 0, swapped).start()
+            straight(j, 1, swapped).start()
+
+        @pl.when(stays)
+        def _():
+            local(j, 0).start()
+            local(j, 1).start()
+
+    def mirror_relay(j):
+        @pl.when(both)
+        def _():
+            to_y(j).wait_recv()
+            second_a(j).start()
+
+        @pl.when(diagonal)
+        def _():
+            for step in range(1, 4):
+                remote(code.at[j, 1], via_z.at[step - 1, j], z_send.at[j], z_recv.at[step - 1, j], opposite).wait_recv()
+                second_b(j, step).start()
+
+    def mirror_wait(j):
+        @pl.when(both)
+        def _():
+            to_y(j).wait_send()
+            second_a(j).wait()
+
+        @pl.when(only_turn)
+        def _():
+            straight(j, 0, flipped).wait()
+
+        @pl.when(turned)
+        def _():
+            to_corner(j).wait_send()
+            straight(j, 1, flipped).wait_recv()
+
+        @pl.when(only_cross)
+        def _():
+            straight(j, 0, swapped).wait()
+            straight(j, 1, swapped).wait()
+
+        @pl.when(stays)
+        def _():
+            local(j, 0).wait()
+            local(j, 1).wait()
+
+        @pl.when(diagonal)
+        def _():
+            for step in range(1, 4):
+                second_b(j, step).wait_send()
 
     finals = []
 
@@ -180,14 +329,7 @@
         )
         pair.start()
 
-        @pl.when(off_diagonal)
-        def _():
-            remote(cyct.at[j], mirror.at[j], x_send.at[j], x_recv.at[j], partner).start()
-
-        @pl.when(jnp.logical_not(off_diagonal))
-        def _():
-            pltpu.make_async_copy(cyct.at[j], mirror.at[j], x_send.at[j]).start()
-
+        mirror_send(j)
         finals.append((own, pair))
 
     t_local = [pltpu.make_async_copy(amp.at[i], tv.at[c * HALF + i], t_own.at[i]) for i in range(HALF)]
@@ -198,6 +340,9 @@
         t_local[i].start()
         t_pair[i].start()
     stage0(1)
+    make_mask()
+    mask_pair.start()
+    mask_own.start()
     stage1(0)
     stage0(2)
     stage1(1)
@@ -229,6 +374,8 @@
     near(2)
     near(3)
     contract(GROUPS[1], False)
+    mirror_relay(0)
+    mirror_relay(1)
     stage2(4)
     rest(2)
     rest(3)
@@ -237,9 +384,12 @@
     hand_out(3)
     near(4)
     contract(GROUPS[2], False)
+    mirror_relay(2)
+    mirror_relay(3)
     rest(4)
     contract(GROUPS[2], True)
     hand_out(4)
+    mirror_relay(4)
 
     for copy in sends:
         copy.wait_send()
@@ -249,49 +399,66 @@
         own.wait()
         pair.wait()
     for j in range(HALF):
-        @pl.when(off_diagonal)
-        def _():
-            remote(cyct.at[j], mirror.at[j], x_send.at[j], x_recv.at[j], partner).wait()
-
-        @pl.when(jnp.logical_not(off_diagonal))
-        def _():
-            pltpu.make_async_copy(cyct.at[j], mirror.at[j], x_send.at[j]).wait()
+        mirror_wait(j)
+
+
+def coded(tile):
+    largest = jnp.max(jnp.max(jnp.abs(tile), axis=0, keepdims=True), axis=1, keepdims=True)
+    scale = jnp.broadcast_to(jnp.maximum(largest, 2.0**-100), (16, TILE)).astype(jnp.bfloat16).astype(jnp.float32)
+    value = tile * (TOP / scale[:1])
+    square = value * value
+    fourth = square * square
+    eighth = fourth * fourth
+    return jnp.where(value < 0, -eighth, eighth).astype(jnp.bfloat16), scale
+
+
+def finish(direct, mirror, out):
+    for half in range(2):
+        scales = mirror[0, half, HALF * TILE : PACK].astype(jnp.float32) * (1 / TOP)
+        for n in range(HALF):
+            value = mirror[0, half, n * TILE : (n + 1) * TILE].astype(jnp.float32)
+            root = jnp.sqrt(jnp.sqrt(jnp.sqrt(jnp.abs(value)))) * scales[n : n + 1]
+            out[0, half * HALF + n] = direct[0, half * HALF + n] + jnp.where(value < 0, -root, root)
 
 
 def on_device(amplitudes, integrals, pair_lists, pair_counts):
-    rows_here, cols_here, slots = pair_lists.shape
-    in_count = jnp.arange(slots, dtype=jnp.int32)[None, None, :] < pair_counts[:, :, None]
-    labels = jnp.arange(TILE, dtype=jnp.int32)
-    live = jnp.any(
-        (pair_lists[:, :, :, None] == labels[None, None, None, :]) & in_count[:, :, :, None], axis=2
-    ).astype(jnp.float32)
-    mask = live.reshape(rows_here, 2, HALF, TILE).transpose(1, 0, 2, 3).reshape(2, HALF * HALF, TILE)
-    mask = jnp.pad(mask, ((0, 0), (0, 32 - HALF * HALF), (0, 0)))
     bf, f32 = jnp.bfloat16, jnp.float32
     dma = pltpu.SemaphoreType.DMA
     tiles = jax.ShapeDtypeStruct((HALF, CHIP, TILE, TILE), f32)
     anywhere = pl.BlockSpec(memory_space=pl.ANY)
     direct, mirror = pl.pallas_call(
         kernel,
-        out_shape=(tiles, tiles),
-        in_specs=[anywhere] * 3,
+        out_shape=(tiles, jax.ShapeDtypeStruct((HALF, 2, PACK, TILE), bf)),
+        in_specs=[anywhere] * 2 + [pl.BlockSpec(memory_space=pltpu.VMEM)] * 2,
         out_specs=(anywhere, anywhere),
         scratch_shapes=[
             pltpu.VMEM((CHIP, O, TILE, TILE), bf),
             pltpu.VMEM((HALF, O, TILE, TILE), bf),
             pltpu.VMEM((HALF, CHIP, TILE, TILE), f32),
-            pltpu.VMEM((HALF, CHIP, TILE, TILE), f32),
-            pltpu.VMEM((32, TILE), f32),
-            pltpu.SMEM((2, 32, TILE), f32),
+            pltpu.VMEM((HALF, 2, PACK, TILE), bf),
+            pltpu.VMEM((HALF, PACK, TILE), bf),
+            pltpu.VMEM((3, HALF, PACK, TILE), bf),
+            pltpu.VMEM((2, 40, TILE), f32),
+            pltpu.VMEM((40, TILE), f32),
+            pltpu.SMEM((2, 40, TILE), f32),
             dma((HALF,)), dma((HALF,)), dma((HALF,)), dma((HALF,)), dma((HALF,)), dma((HALF,)), dma((3,)),
-            dma((70,)), dma((70,)), dma((HALF,)), dma((HALF,)), dma((HALF,)), dma((HALF,)), dma((HALF,)),
+            dma((70,)), dma((70,)), dma((HALF,)), dma((HALF,)), dma((HALF,)),
+            dma((HALF,)), dma((HALF,)), dma((HALF,)), dma((3, HALF)), dma((HALF,)), dma((HALF,)), dma((HALF,)), dma((HALF,)), dma((3, HALF)),
         ],
         compiler_params=pltpu.CompilerParams(
             collective_id=0, has_side_effects=True, vmem_limit_bytes=60 * 1024 * 1024
         ),
         cost_estimate=pl.CostEstimate(flops=17_000_000_000, bytes_accessed=60_000_000, transcendentals=0),
-    )(amplitudes, integrals, mask)
-    return direct + mirror
+    )(amplitudes, integrals, pair_lists, pair_counts)
+    ten = pl.BlockSpec((1, CHIP, TILE, TILE), lambda i: (i, 0, 0, 0))
+    return pl.pallas_call(
+        finish,
+        grid=(HALF,),
+        out_shape=tiles,
+        in_specs=[ten, pl.BlockSpec((1, 2, PACK, TILE), lambda i: (i, 0, 0, 0))],
+        out_specs=ten,
+        compiler_params=pltpu.CompilerParams(vmem_limit_bytes=60 * 1024 * 1024),
+    )(direct, mirror)
 
 
 def solution(mesh):

time: 362 us -> 150 us (0.41)
  the two profiles are of different devices: /device:TPU:8 before, /device:TPU:28 now
where the time goes in v2:
time: 150 us
  Pallas kernels  150 us (100%)
    pallas_call x1, Pallas kernels, on_device(): pl.pallas_call(kernel, out_shape=(tiles, jax.ShapeDtypeStruct((HALF, 2, P...  143 us
    pallas_call x1, Pallas kernels, on_device(): pl.pallas_call(finish, grid=(HALF,), out_shape=tiles, in_specs=[ten, pl.B...  6.69 us

profile of v2, /device:TPU:28, one launch (start us, length us, event | category | flops | bytes accessed | tf_op | source)
XLA Modules:
  0.0 150.1 jit_solution(3161602090824434687)
XLA Ops:
  0.0 143.4 %shard_map.46 = (f32[5,10,128,128]{3,2,1,0:T(8,128)}, bf16[5,2,656,128]{3,2,1,0:T(8,128)(2,1)}) custom-call(bf16[5,80,128,128]{3,2,1,0:T(8,128)(2,1)} %amp.1, bf16[5,10,128,128]{3,2,1,0:T(8,128)(2,1)} %integ.1, s32[5,10,48]{2,1,0:T(8,128)} %lists.1, s32[5,10]{1,0:T(8,128)} %counts.1), custom_call_target="tpu_custom_call" | custom-call | flops 16999999488 | bytes 60000000 | tf_op jit(solution)/shard_map/pallas_call | solution.py:429
  143.4 6.7 %shard_map.47 = f32[5,10,128,128]{3,2,1,0:T(8,128)} custom-call(f32[5,10,128,128]{3,2,1,0:T(8,128)} %get-tuple-element.7.direct, bf16[5,2,656,128]{3,2,1,0:T(8,128)(2,1)} %get-tuple-element.8.mirror), custom_call_target="tpu_custom_call" | custom-call | tf_op jit(solution)/shard_map/pallas_call | solution.py:454

commit v3 on v2

--- a/solution.py
+++ b/solution.py
@@ -12,18 +12,21 @@
 O = 80
 HALF = 5
 CHIP = 10
-GROUPS = ((0, 1), (2, 3), (4,))
-PACK = HALF * TILE + 16
+Y_FIRST = ((1, 1, 1, 1, 1), (0, 0, 0, 0, 0))
+PACK = HALF * TILE + 32
+LEG = PACK // 2
+SIGNS = (1, -1)
 TOP = 2.0**15
 Y, BACK, FRONT, FAR, BACK_Y, FRONT_Y, FAR_Y = range(7)
 
 
 def kernel(
     amp, integ, lists, counts, direct, mirror,
-    tv, wv, cyc, code, via_y, via_z, mine_v, mv, ms,
+    tv, wv, cyc, code, via_y, via_z, via_s, via_e, mine_v, mv, ms,
     own_sem, pair_send, pair_recv, t_own, t_send, t_recv, m_sem,
     g_send, g_recv, d_own, d_send, d_recv,
     y_send, y_recv, z_send, z_recv, a_send, a_recv, b_send, b_recv, c_send,
+    s_send, s_recv, sa_send, sa_recv, e_send, e_recv, e1_send, eb_recv,
 ):
     row, col = lax.axis_index("row"), lax.axis_index("col")
     z, y, c = row // 4, (row // 2) % 2, row % 2
@@ -41,15 +44,24 @@
 
     crossing = y != y_hi
     diagonal = delta == 0
-    turned = jnp.logical_not(diagonal)
+    turned = lax.rem(delta, 2) == 1
+    across = delta == 2
+    sign = jnp.where(delta == 3, 1, -1)
+    side = jnp.where(delta == 3, 0, 1)
     stays = jnp.logical_and(diagonal, jnp.logical_not(crossing))
     swapped = at(x, y_hi, y, z)
     flipped = at(z, y, y_hi, x)
     corner = at(x, y, y_hi, x)
-    opposite = at(x, y, y_hi, lax.rem(z + 2, 4))
 
     def block(dz, dy):
         return lax.rem(z + dz + 4, 4) * 2 + (y if dy == 0 else 1 - y)
+
+    def near_x(step):
+        return at(lax.rem(x + step + 4, 4), y, y_hi, z)
+
+    def aslant(step, cross):
+        lo, hi = (y_hi, y) if cross else (y, y_hi)
+        return at(lax.rem(x + step + 4, 4), lo, hi, lax.rem(z + step + 4, 4))
 
     barrier = pltpu.get_barrier_semaphore()
 
@@ -67,18 +79,28 @@
     def _():
         greet(flipped)
         greet(at(z, y_hi, y, z))
-
-    @pl.when(lax.rem(delta, 2) == 0)
+        greet(near_x(sign))
+        greet(aslant(sign, True))
+        greet(aslant(-sign, True))
+
+    @pl.when(across)
     def _():
-        greet(opposite)
+        for step in SIGNS:
+            greet(near_x(step))
+            greet(aslant(step, False))
+
+    @pl.when(jnp.logical_and(across, crossing))
+    def _():
+        for step in SIGNS:
+            greet(aslant(step, True))
 
     @pl.when(diagonal)
     def _():
-        for step in range(1, 4):
+        for step in (1, 3):
             greet(at(lax.rem(x + step, 4), y_hi, y, z))
 
     peers = (
-        4 + jnp.where(crossing, 1, 0) + jnp.where(turned, 2, 3) + jnp.where(lax.rem(delta, 2) == 0, 1, 0)
+        4 + jnp.where(crossing, 1, 0) + jnp.where(turned, 5, jnp.where(across, jnp.where(crossing, 6, 4), 2))
     )
     pl.semaphore_wait(barrier, peers)
 
@@ -117,75 +139,86 @@
             for half in range(2):
                 mine_v[half, i * 8 : i * 8 + HALF] = live[half * HALF : (half + 1) * HALF]
 
-    def piece(kind, j, dz, dy):
-        part = c if kind == 0 else other
-        view = pl.ds(block(dz, dy) * CHIP + part * HALF, HALF)
+    def piece(part, j, dz, dy):
+        view = pl.ds(block(dz, dy) * CHIP + (c if part == 0 else other) * HALF, HALF)
         return wv.at[j, view]
 
     sends = []
 
-    def send(kind, j, dz, dy, name, device):
-        ref = piece(kind, j, dz, dy)
-        slot = (j * 2 + kind) * 7 + name
+    def send(part, j, dz, dy, name, device):
+        ref = piece(part, j, dz, dy)
+        slot = (j * 2 + part) * 7 + name
         copy = remote(ref, ref, g_send.at[slot], g_recv.at[slot], device)
         copy.start()
         sends.append(copy)
 
-    def arrived(kind, j, name):
-        far = 1 if (kind + j) % 2 == 0 else -1
+    def arrived(part, j, name):
+        far = ahead(part, j)[2]
         dz, dy = {
             Y: (0, 1), BACK: (-far, 0), FRONT: (far, 0), FAR: (2, 0),
             BACK_Y: (-far, 1), FRONT_Y: (far, 1), FAR_Y: (2, 1),
         }[name]
-        ref = piece(kind, j, dz, dy)
-        slot = (j * 2 + kind) * 7 + name
+        ref = piece(part, j, dz, dy)
+        slot = (j * 2 + part) * 7 + name
         remote(ref, ref, g_send.at[slot], g_recv.at[slot], y_dev).wait_recv()
 
-    def ahead(kind, j):
-        plus = (kind + j) % 2 == 0
-        return (up, down, 1) if plus else (down, up, -1)
+    def ahead(part, j):
+        return (up, down, 1) if (part + j) % 2 == 0 else (down, up, -1)
+
+    def own(part, j):
+        front, back, far = ahead(part, j)
+        if part == 0:
+            own_w[j].wait()
+        else:
+            pair_w[j].wait_recv()
+        send(part, j, 0, 0, BACK, front)
+        send(part, j, 0, 0, FRONT, back)
+        send(part, j, 0, 0, Y, y_dev)
+
+    def first(part, j):
+        front, back, far = ahead(part, j)
+        if Y_FIRST[part][j]:
+            arrived(part, j, Y)
+            send(part, j, 0, 1, BACK_Y, front)
+            send(part, j, 0, 1, FRONT_Y, back)
+            arrived(part, j, BACK)
+            send(part, j, -far, 0, FAR, front)
+        else:
+            arrived(part, j, BACK)
+            send(part, j, -far, 0, FAR, front)
+            send(part, j, -far, 0, BACK_Y, y_dev)
+            arrived(part, j, FRONT)
+            send(part, j, far, 0, FRONT_Y, y_dev)
+
+    def second(part, j):
+        front, back, far = ahead(part, j)
+        if Y_FIRST[part][j]:
+            arrived(part, j, BACK_Y)
+            send(part, j, -far, 1, FAR_Y, front)
+        else:
+            arrived(part, j, FAR)
+            send(part, j, 2, 0, FAR_Y, y_dev)
+
+    def near(j):
+        for part in range(2):
+            arrived(part, j, FRONT if Y_FIRST[part][j] else Y)
+
+    def rest(j):
+        for part in range(2):
+            for name in (FRONT_Y, FAR, FAR_Y) if Y_FIRST[part][j] else (BACK_Y, FRONT_Y, FAR_Y):
+                arrived(part, j, name)
 
     def stage0(j):
-        for kind in range(2):
-            front, back, far = ahead(kind, j)
-            if kind == 0:
-                own_w[j].wait()
-            else:
-                pair_w[j].wait_recv()
-            send(kind, j, 0, 0, BACK, front)
-            send(kind, j, 0, 0, FRONT, back)
-            send(kind, j, 0, 0, Y, y_dev)
+        own(0, j)
+        own(1, j)
 
     def stage1(j):
-        front, back, far = ahead(0, j)
-        arrived(0, j, Y)
-        send(0, j, 0, 1, BACK_Y, front)
-        send(0, j, 0, 1, FRONT_Y, back)
-        arrived(0, j, BACK)
-        send(0, j, -far, 0, FAR, front)
-        front, back, far = ahead(1, j)
-        arrived(1, j, BACK)
-        send(1, j, -far, 0, FAR, front)
-        send(1, j, -far, 0, BACK_Y, y_dev)
-        arrived(1, j, FRONT)
-        send(1, j, far, 0, FRONT_Y, y_dev)
+        first(0, j)
+        first(1, j)
 
     def stage2(j):
-        front, back, far = ahead(0, j)
-        arrived(0, j, BACK_Y)
-        send(0, j, -far, 1, FAR_Y, front)
-        arrived(1, j, FAR)
-        send(1, j, 2, 0, FAR_Y, y_dev)
-
-    def near(j):
-        arrived(0, j, FRONT)
-        arrived(1, j, Y)
-
-    def rest(j):
-        for name in (FRONT_Y, FAR, FAR_Y):
-            arrived(0, j, name)
-        for name in (BACK_Y, FRONT_Y, FAR_Y):
-            arrived(1, j, name)
+        second(0, j)
+        second(1, j)
 
     def contract(js, late):
         places = ((1, 1), (-1, 1), (2, 0), (2, 1)) if late else ((0, 0), (0, 1), (1, 0), (-1, 0))
@@ -223,7 +256,7 @@
             for n, j in enumerate(js):
                 for half in range(2):
                     part = scales[n][half * 8 : half * 8 + 8]
-                    code[j, half, HALF * TILE : PACK] = jnp.concatenate([part, part], axis=0).astype(jnp.bfloat16)
+                    code[j, half, HALF * TILE : PACK] = jnp.concatenate([part] * 4, axis=0).astype(jnp.bfloat16)
 
     def mirror_half(j, half):
         return mirror.at[j, half]
@@ -250,6 +283,31 @@
         device = at(lax.rem(x + step, 4), y_hi, y, z)
         return remote(via_z.at[step - 1, j], mirror_half(j, 1), c_send.at[step - 1, j], b_recv.at[j], device)
 
+    def leg(d):
+        return pl.ds(d * LEG, LEG)
+
+    def slant_out(j, d):
+        return remote(
+            code.at[j, 0, leg(d)], via_s.at[d, j], s_send.at[d, j], s_recv.at[d, j], aslant(SIGNS[d], True)
+        )
+
+    def slant_in(j, d):
+        return remote(
+            via_s.at[d, j], mirror.at[j, 0, leg(d)], sa_send.at[d, j], sa_recv.at[d, j], aslant(SIGNS[d], False)
+        )
+
+    def edge_out(j, d):
+        return remote(
+            code.at[j, 1, leg(d)], via_e.at[0, j], e_send.at[d, j], e_recv.at[0, j], up if d == 0 else down
+        )
+
+    def edge_mid(j):
+        return remote(via_e.at[0, j], via_e.at[1, j], e1_send.at[0, j], e_recv.at[1, j], aslant(sign, True))
+
+    def edge_in(j):
+        rows = pl.ds(pl.multiple_of(side * LEG, 16), LEG)
+        return remote(via_e.at[1, j], mirror.at[j, 1, rows], e1_send.at[1, j], eb_recv.at[side, j], near_x(sign))
+
     both = jnp.logical_and(crossing, turned)
     only_cross = jnp.logical_and(crossing, diagonal)
     only_turn = jnp.logical_and(jnp.logical_not(crossing), turned)
@@ -267,6 +325,12 @@
         def _():
             to_corner(j).start()
 
+        @pl.when(across)
+        def _():
+            for d in range(2):
+                slant_out(j, d).start()
+                edge_out(j, d).start()
+
         @pl.when(only_cross)
         def _():
             straight(j, 0, swapped).start()
@@ -285,11 +349,43 @@
 
         @pl.when(diagonal)
         def _():
-            for step in range(1, 4):
-                remote(code.at[j, 1], via_z.at[step - 1, j], z_send.at[j], z_recv.at[step - 1, j], opposite).wait_recv()
+            for step in (1, 3):
+                remote(code.at[j, 1], via_z.at[step - 1, j], z_send.at[j], z_recv.at[step - 1, j], sibling).wait_recv()
                 second_b(j, step).start()
 
+        @pl.when(across)
+        def _():
+            for d in range(2):
+                slant_out(j, d).wait_recv()
+                slant_in(j, d).start()
+
+        @pl.when(turned)
+        def _():
+            edge_out(j, 0).wait_recv()
+            edge_mid(j).start()
+
+    def mirror_last(j):
+        @pl.when(turned)
+        def _():
+            edge_mid(j).wait_recv()
+            edge_in(j).start()
+
     def mirror_wait(j):
+        @pl.when(across)
+        def _():
+            for d in range(2):
+                slant_out(j, d).wait_send()
+                slant_in(j, d).wait()
+                edge_out(j, d).wait_send()
+                remote(
+                    code.at[j, 1, leg(d)], mirror.at[j, 1, leg(d)], e_send.at[d, j], eb_recv.at[d, j], sibling
+                ).wait_recv()
+
+        @pl.when(turned)
+        def _():
+            edge_mid(j).wait_send()
+            edge_in(j).wait_send()
+
         @pl.when(both)
         def _():
             to_y(j).wait_send()
@@ -316,21 +412,21 @@
 
         @pl.when(diagonal)
         def _():
-            for step in range(1, 4):
+            for step in (1, 3):
                 second_b(j, step).wait_send()
 
     finals = []
 
     def hand_out(j):
-        own = pltpu.make_async_copy(cyc.at[j, pl.ds(c * HALF, HALF)], direct.at[:, c * HALF + j], d_own.at[j])
-        own.start()
+        keep = pltpu.make_async_copy(cyc.at[j, pl.ds(c * HALF, HALF)], direct.at[:, c * HALF + j], d_own.at[j])
+        keep.start()
         pair = remote(
             cyc.at[j, pl.ds(other * HALF, HALF)], direct.at[:, c * HALF + j], d_send.at[j], d_recv.at[j], sibling
         )
         pair.start()
 
         mirror_send(j)
-        finals.append((own, pair))
+        finals.append((keep, pair))
 
     t_local = [pltpu.make_async_copy(amp.at[i], tv.at[c * HALF + i], t_own.at[i]) for i in range(HALF)]
     t_pair = [remote(amp.at[i], tv.at[c * HALF + i], t_send.at[i], t_recv.at[i], sibling) for i in range(HALF)]
@@ -344,59 +440,68 @@
     mask_pair.start()
     mask_own.start()
     stage1(0)
-    stage0(2)
-    stage1(1)
     stage2(0)
-    stage0(3)
-    stage1(2)
-    stage2(1)
-    near(0)
-    near(1)
     mask_pair.wait()
     mask_own.wait()
-    second = pltpu.make_async_copy(mv, ms.at[other], m_sem.at[2])
-    second.start()
-    second.wait()
+    mask_theirs = pltpu.make_async_copy(mv, ms.at[other], m_sem.at[2])
+    mask_theirs.start()
+    mask_theirs.wait()
     for i in range(HALF):
         t_local[i].wait()
         t_pair[i].wait()
-    contract(GROUPS[0], False)
+    stage1(1)
+    stage0(2)
+    near(0)
+    contract((0,), False)
+    rest(0)
+    contract((0,), True)
+    hand_out(0)
+    stage2(1)
+    stage1(2)
+    stage0(3)
+    near(1)
+    contract((1,), False)
+    rest(1)
+    contract((1,), True)
+    hand_out(1)
+    mirror_relay(0)
+    stage2(2)
+    stage1(3)
     stage0(4)
-    stage1(3)
-    stage2(2)
-    rest(0)
-    rest(1)
-    contract(GROUPS[0], True)
-    hand_out(0)
-    hand_out(1)
+    near(2)
+    contract((2,), False)
+    rest(2)
+    contract((2,), True)
+    hand_out(2)
+    mirror_relay(1)
+    mirror_last(0)
+    stage2(3)
     stage1(4)
-    stage2(3)
-    near(2)
     near(3)
-    contract(GROUPS[1], False)
-    mirror_relay(0)
-    mirror_relay(1)
+    contract((3,), False)
+    rest(3)
+    contract((3,), True)
+    hand_out(3)
+    mirror_relay(2)
+    mirror_last(1)
     stage2(4)
-    rest(2)
-    rest(3)
-    contract(GROUPS[1], True)
-    hand_out(2)
-    hand_out(3)
     near(4)
-    contract(GROUPS[2], False)
-    mirror_relay(2)
+    contract((4,), False)
     mirror_relay(3)
+    mirror_last(2)
     rest(4)
-    contract(GROUPS[2], True)
+    contract((4,), True)
     hand_out(4)
     mirror_relay(4)
+    mirror_last(3)
+    mirror_last(4)
 
     for copy in sends:
         copy.wait_send()
     for copy in pair_w:
         copy.wait_send()
-    for own, pair in finals:
-        own.wait()
+    for keep, pair in finals:
+        keep.wait()
         pair.wait()
     for j in range(HALF):
         mirror_wait(j)
@@ -438,12 +543,15 @@
             pltpu.VMEM((HALF, 2, PACK, TILE), bf),
             pltpu.VMEM((HALF, PACK, TILE), bf),
             pltpu.VMEM((3, HALF, PACK, TILE), bf),
+            pltpu.VMEM((2, HALF, LEG, TILE), bf),
+            pltpu.VMEM((2, HALF, LEG, TILE), bf),
             pltpu.VMEM((2, 40, TILE), f32),
             pltpu.VMEM((40, TILE), f32),
             pltpu.SMEM((2, 40, TILE), f32),
             dma((HALF,)), dma((HALF,)), dma((HALF,)), dma((HALF,)), dma((HALF,)), dma((HALF,)), dma((3,)),
             dma((70,)), dma((70,)), dma((HALF,)), dma((HALF,)), dma((HALF,)),
             dma((HALF,)), dma((HALF,)), dma((HALF,)), dma((3, HALF)), dma((HALF,)), dma((HALF,)), dma((HALF,)), dma((HALF,)), dma((3, HALF)),
+            dma((2, HALF)), dma((2, HALF)), dma((2, HALF)), dma((2, HALF)), dma((2, HALF)), dma((2, HALF)), dma((2, HALF)), dma((2, HALF)),
         ],
         compiler_params=pltpu.CompilerParams(
             collective_id=0, has_side_effects=True, vmem_limit_bytes=60 * 1024 * 1024

time: 150 us -> 143 us (0.953)
  the two profiles are of different devices: /device:TPU:28 before, /device:TPU:72 now
where the time goes in v3:
time: 143 us
  Pallas kernels  143 us (100%)
    pallas_call x1, Pallas kernels, on_device(): pl.pallas_call(kernel, out_shape=(tiles, jax.ShapeDtypeStruct((HALF, 2, P...  136 us
    pallas_call x1, Pallas kernels, on_device(): pl.pallas_call(finish, grid=(HALF,), out_shape=tiles, in_specs=[ten, pl.B...  6.7 us

profile of v3, /device:TPU:72, one launch (start us, length us, event | category | flops | bytes accessed | tf_op | source)
XLA Modules:
  0.0 142.6 jit_solution(8632610888586141655)
XLA Ops:
  0.0 135.9 %shard_map.46 = (f32[5,10,128,128]{3,2,1,0:T(8,128)}, bf16[5,2,672,128]{3,2,1,0:T(8,128)(2,1)}) custom-call(bf16[5,80,128,128]{3,2,1,0:T(8,128)(2,1)} %amp.1, bf16[5,10,128,128]{3,2,1,0:T(8,128)(2,1)} %integ.1, s32[5,10,48]{2,1,0:T(8,128)} %lists.1, s32[5,10]{1,0:T(8,128)} %counts.1), custom_call_target="tpu_custom_call" | custom-call | flops 16999999488 | bytes 60000000 | tf_op jit(solution)/shard_map/pallas_call | solution.py:534
  135.9 6.7 %shard_map.47 = f32[5,10,128,128]{3,2,1,0:T(8,128)} custom-call(f32[5,10,128,128]{3,2,1,0:T(8,128)} %get-tuple-element.7.direct, bf16[5,2,672,128]{3,2,1,0:T(8,128)(2,1)} %get-tuple-element.8.mirror), custom_call_target="tpu_custom_call" | custom-call | tf_op jit(solution)/shard_map/pallas_call | solution.py:562

commit v4 on v3

--- a/solution.py
+++ b/solution.py
@@ -148,9 +148,14 @@
     def send(part, j, dz, dy, name, device):
         ref = piece(part, j, dz, dy)
         slot = (j * 2 + part) * 7 + name
-        copy = remote(ref, ref, g_send.at[slot], g_recv.at[slot], device)
-        copy.start()
-        sends.append(copy)
+        src = integ.at[:, c * HALF + j] if part == 0 and (dz, dy) == (0, 0) else ref
+        remote(src, ref, g_send.at[slot], g_recv.at[slot], device).start()
+        sends.append((part, j, dz, dy, name, device))
+
+    def sent(part, j, dz, dy, name, device):
+        ref = piece(part, j, dz, dy)
+        slot = (j * 2 + part) * 7 + name
+        remote(ref, ref, g_send.at[slot], g_recv.at[slot], device).wait_send()
 
     def arrived(part, j, name):
         far = ahead(part, j)[2]
@@ -167,9 +172,7 @@
 
     def own(part, j):
         front, back, far = ahead(part, j)
-        if part == 0:
-            own_w[j].wait()
-        else:
+        if part == 1:
             pair_w[j].wait_recv()
         send(part, j, 0, 0, BACK, front)
         send(part, j, 0, 0, FRONT, back)
@@ -200,13 +203,18 @@
             send(part, j, 2, 0, FAR_Y, y_dev)
 
     def near(j):
+        own_w[j].wait()
         for part in range(2):
             arrived(part, j, FRONT if Y_FIRST[part][j] else Y)
 
     def rest(j):
         for part in range(2):
-            for name in (FRONT_Y, FAR, FAR_Y) if Y_FIRST[part][j] else (BACK_Y, FRONT_Y, FAR_Y):
+            for name in (FRONT_Y, FAR) if Y_FIRST[part][j] else (BACK_Y, FRONT_Y):
                 arrived(part, j, name)
+
+    def last(j):
+        for part in range(2):
+            arrived(part, j, FAR_Y)
 
     def stage0(j):
         own(0, j)
@@ -220,43 +228,54 @@
         second(0, j)
         second(1, j)
 
-    def contract(js, late):
-        places = ((1, 1), (-1, 1), (2, 0), (2, 1)) if late else ((0, 0), (0, 1), (1, 0), (-1, 0))
+    near_places = ((0, 0), (0, 1), (1, 0), (-1, 0))
+    rest_places = ((1, 1), (-1, 1), (2, 0))
+    last_places = ((2, 1),)
+
+    def contract(j, places, i_from, i_to, final, hooks):
         starts = [block(dz, dy) * CHIP for dz, dy in places]
         labels = [start + k for start in starts for k in range(CHIP)]
-
-        def one(i, carry):
+        opening = places[0] == (0, 0)
+
+        def one(i, scales):
+            for step, hook in hooks.items():
+                pl.when(i == step)(hook)
             left = jnp.concatenate([tv[i, k] for k in labels], axis=1)
-            right = []
-            for j in js:
-                right.append(
-                    jnp.concatenate(
-                        [
-                            wv[j, k] * jnp.full((TILE, TILE), ms[i // HALF, lax.rem(i, HALF) * 8 + j, k], jnp.float32).astype(jnp.bfloat16)
-                            for k in labels
-                        ],
-                        axis=0,
-                    )
-                )
-            right = right[0] if len(js) == 1 else jnp.concatenate(right, axis=1)
-            out = jnp.dot(left, right, preferred_element_type=jnp.float32)
-            for n, j in enumerate(js):
-                tile = out[:, n * TILE : (n + 1) * TILE]
-                if late:
-                    tile = tile + cyc[j, i]
-                    packed, scale = coded(tile.T)
-                    code[j, i // HALF, pl.ds(pl.multiple_of(lax.rem(i, HALF) * TILE, TILE), TILE)] = packed
-                    carry = carry[:n] + (jnp.where(rows == i + (i // HALF) * 3, scale, carry[n]),) + carry[n + 1 :]
-                cyc[j, i] = tile
-            return carry
-
-        rows = lax.broadcasted_iota(jnp.int32, (16, TILE), 0)
-        scales = lax.fori_loop(0, CHIP, one, tuple(jnp.zeros((16, TILE), jnp.float32) for _ in js))
-        if late:
-            for n, j in enumerate(js):
-                for half in range(2):
-                    part = scales[n][half * 8 : half * 8 + 8]
-                    code[j, half, HALF * TILE : PACK] = jnp.concatenate([part] * 4, axis=0).astype(jnp.bfloat16)
+            right = jnp.concatenate(
+                [
+                    wv[j, k]
+                    * jnp.full((TILE, TILE), ms[i // HALF, lax.rem(i, HALF) * 8 + j, k], jnp.float32).astype(jnp.bfloat16)
+                    for k in labels
+                ],
+                axis=0,
+            )
+            tile = jnp.dot(left, right, preferred_element_type=jnp.float32)
+            if not opening:
+                tile = tile + cyc[j, i]
+            if final:
+                n = i - i_from
+                packed, scale = coded(tile.T)
+                code[j, i_from // HALF, pl.ds(pl.multiple_of(n * TILE, TILE), TILE)] = packed
+                scales = jnp.where(rows == n, scale[:8], scales)
+            cyc[j, i] = tile
+            return scales
+
+        rows = lax.broadcasted_iota(jnp.int32, (8, TILE), 0)
+        scales = lax.fori_loop(i_from, i_to, one, jnp.zeros((8, TILE), jnp.float32))
+        if final:
+            code[j, i_from // HALF, HALF * TILE : PACK] = jnp.concatenate([scales] * 4, axis=0).astype(jnp.bfloat16)
+
+    def begin(j, hooks):
+        contract(j, near_places, 0, CHIP, False, hooks)
+
+    def carry_on(j, hooks):
+        contract(j, rest_places, 0, CHIP, False, hooks)
+
+    def end(j, places, hooks):
+        for half in range(2):
+            contract(j, places, half * HALF, (half + 1) * HALF, True, hooks)
+            mirror_send(j, half)
+        hand_out(j)
 
     def mirror_half(j, half):
         return mirror.at[j, half]
@@ -312,34 +331,19 @@
     only_cross = jnp.logical_and(crossing, diagonal)
     only_turn = jnp.logical_and(jnp.logical_not(crossing), turned)
 
-    def mirror_send(j):
-        @pl.when(both)
-        def _():
-            to_y(j).start()
-
-        @pl.when(only_turn)
-        def _():
-            straight(j, 0, flipped).start()
-
-        @pl.when(turned)
-        def _():
-            to_corner(j).start()
+    def mirror_send(j, half):
+        if half == 0:
+            pl.when(both)(lambda: to_y(j).start())
+            pl.when(only_turn)(lambda: straight(j, 0, flipped).start())
+        else:
+            pl.when(turned)(lambda: to_corner(j).start())
+        pl.when(only_cross)(lambda: straight(j, half, swapped).start())
+        pl.when(stays)(lambda: local(j, half).start())
 
         @pl.when(across)
         def _():
             for d in range(2):
-                slant_out(j, d).start()
-                edge_out(j, d).start()
-
-        @pl.when(only_cross)
-        def _():
-            straight(j, 0, swapped).start()
-            straight(j, 1, swapped).start()
-
-        @pl.when(stays)
-        def _():
-            local(j, 0).start()
-            local(j, 1).start()
+                (slant_out if half == 0 else edge_out)(j, d).start()
 
     def mirror_relay(j):
         @pl.when(both)
@@ -425,7 +429,6 @@
         )
         pair.start()
 
-        mirror_send(j)
         finals.append((keep, pair))
 
     t_local = [pltpu.make_async_copy(amp.at[i], tv.at[c * HALF + i], t_own.at[i]) for i in range(HALF)]
@@ -452,52 +455,52 @@
     stage1(1)
     stage0(2)
     near(0)
-    contract((0,), False)
+    begin(0, {})
     rest(0)
-    contract((0,), True)
-    hand_out(0)
+    last(0)
+    end(0, rest_places + last_places, {})
     stage2(1)
     stage1(2)
     stage0(3)
     near(1)
-    contract((1,), False)
+    begin(1, {})
     rest(1)
-    contract((1,), True)
-    hand_out(1)
+    last(1)
+    end(1, rest_places + last_places, {})
     mirror_relay(0)
     stage2(2)
     stage1(3)
     stage0(4)
     near(2)
-    contract((2,), False)
+    begin(2, {})
     rest(2)
-    contract((2,), True)
-    hand_out(2)
+    last(2)
+    end(2, rest_places + last_places, {})
     mirror_relay(1)
     mirror_last(0)
     stage2(3)
     stage1(4)
     near(3)
-    contract((3,), False)
+    begin(3, {})
     rest(3)
-    contract((3,), True)
-    hand_out(3)
+    last(3)
+    end(3, rest_places + last_places, {})
     mirror_relay(2)
     mirror_last(1)
     stage2(4)
     near(4)
-    contract((4,), False)
+    begin(4, {})
     mirror_relay(3)
     mirror_last(2)
     rest(4)
-    contract((4,), True)
-    hand_out(4)
+    last(4)
+    end(4, rest_places + last_places, {})
+    mirror_last(3)
     mirror_relay(4)
-    mirror_last(3)
     mirror_last(4)
 
-    for copy in sends:
-        copy.wait_send()
+    for way in sends:
+        sent(*way)
     for copy in pair_w:
         copy.wait_send()
     for keep, pair in finals:
@@ -522,7 +525,9 @@
         scales = mirror[0, half, HALF * TILE : PACK].astype(jnp.float32) * (1 / TOP)
         for n in range(HALF):
             value = mirror[0, half, n * TILE : (n + 1) * TILE].astype(jnp.float32)
-            root = jnp.sqrt(jnp.sqrt(jnp.sqrt(jnp.abs(value)))) * scales[n : n + 1]
+            inverse = lax.rsqrt(jnp.maximum(jnp.abs(value), 2.0**-126))
+            quarter = lax.rsqrt(inverse)
+            root = quarter * lax.rsqrt(quarter) * scales[n : n + 1]
             out[0, half * HALF + n] = direct[0, half * HALF + n] + jnp.where(value < 0, -root, root)
 
 

time: 143 us -> 137 us (0.958)
  the two profiles are of different devices: /device:TPU:72 before, /device:TPU:28 now
where the time goes in v4:
time: 137 us; the launch traced here: 135 us
  Pallas kernels  135 us (99%)
    pallas_call x1, Pallas kernels, on_device(): pl.pallas_call(kernel, out_shape=(tiles, jax.ShapeDtypeStruct((HALF, 2, P...  128 us
    pallas_call x1, Pallas kernels, on_device(): pl.pallas_call(finish, grid=(HALF,), out_shape=tiles, in_specs=[ten, pl.B...  6.22 us

profile of v4, /device:TPU:28, one launch (start us, length us, event | category | flops | bytes accessed | tf_op | source)
XLA Modules:
  0.0 134.6 jit_solution(14470184321341704947)
XLA Ops:
  0.0 128.4 %shard_map.46 = (f32[5,10,128,128]{3,2,1,0:T(8,128)}, bf16[5,2,672,128]{3,2,1,0:T(8,128)(2,1)}) custom-call(bf16[5,80,128,128]{3,2,1,0:T(8,128)(2,1)} %amp.1, bf16[5,10,128,128]{3,2,1,0:T(8,128)(2,1)} %integ.1, s32[5,10,48]{2,1,0:T(8,128)} %lists.1, s32[5,10]{1,0:T(8,128)} %counts.1), custom_call_target="tpu_custom_call" | custom-call | flops 16999999488 | bytes 60000000 | tf_op jit(solution)/shard_map/pallas_call | solution.py:539
  128.4 6.2 %shard_map.47 = f32[5,10,128,128]{3,2,1,0:T(8,128)} custom-call(f32[5,10,128,128]{3,2,1,0:T(8,128)} %get-tuple-element.7.direct, bf16[5,2,672,128]{3,2,1,0:T(8,128)(2,1)} %get-tuple-element.8.mirror), custom_call_target="tpu_custom_call" | custom-call | tf_op jit(solution)/shard_map/pallas_call | solution.py:567

commit v5 on v4

--- a/solution.py
+++ b/solution.py
@@ -275,6 +275,8 @@
         for half in range(2):
             contract(j, places, half * HALF, (half + 1) * HALF, True, hooks)
             mirror_send(j, half)
+            if j == HALF - 1 and half == 0:
+                mirror_last(j - 1)
         hand_out(j)
 
     def mirror_half(j, half):
@@ -464,38 +466,37 @@
     stage0(3)
     near(1)
     begin(1, {})
+    mirror_relay(0)
     rest(1)
     last(1)
     end(1, rest_places + last_places, {})
-    mirror_relay(0)
+    mirror_last(0)
     stage2(2)
     stage1(3)
     stage0(4)
     near(2)
     begin(2, {})
+    mirror_relay(1)
     rest(2)
     last(2)
     end(2, rest_places + last_places, {})
-    mirror_relay(1)
-    mirror_last(0)
+    mirror_last(1)
     stage2(3)
     stage1(4)
     near(3)
     begin(3, {})
+    mirror_relay(2)
     rest(3)
     last(3)
     end(3, rest_places + last_places, {})
-    mirror_relay(2)
-    mirror_last(1)
+    mirror_last(2)
     stage2(4)
     near(4)
     begin(4, {})
     mirror_relay(3)
-    mirror_last(2)
     rest(4)
     last(4)
     end(4, rest_places + last_places, {})
-    mirror_last(3)
     mirror_relay(4)
     mirror_last(4)
 

time: 137 us -> 134 us (0.978); the launches traced: 135 us -> 134 us
  no operation moved by 1% of the time
where the time goes in v5:
time: 134 us
  Pallas kernels  134 us (100%)
    pallas_call x1, Pallas kernels, on_device(): pl.pallas_call(kernel, out_shape=(tiles, jax.ShapeDtypeStruct((HALF, 2, P...  128 us
    pallas_call x1, Pallas kernels, on_device(): pl.pallas_call(finish, grid=(HALF,), out_shape=tiles, in_specs=[ten, pl.B...  6.22 us

profile of v5, /device:TPU:28, one launch (start us, length us, event | category | flops | bytes accessed | tf_op | source)
XLA Modules:
  0.0 133.8 jit_solution(9490810143169222722)
XLA Ops:
  0.0 127.6 %shard_map.46 = (f32[5,10,128,128]{3,2,1,0:T(8,128)}, bf16[5,2,672,128]{3,2,1,0:T(8,128)(2,1)}) custom-call(bf16[5,80,128,128]{3,2,1,0:T(8,128)(2,1)} %amp.1, bf16[5,10,128,128]{3,2,1,0:T(8,128)(2,1)} %integ.1, s32[5,10,48]{2,1,0:T(8,128)} %lists.1, s32[5,10]{1,0:T(8,128)} %counts.1), custom_call_target="tpu_custom_call" | custom-call | flops 16999999488 | bytes 60000000 | tf_op jit(solution)/shard_map/pallas_call | solution.py:540
  127.6 6.2 %shard_map.47 = f32[5,10,128,128]{3,2,1,0:T(8,128)} custom-call(f32[5,10,128,128]{3,2,1,0:T(8,128)} %get-tuple-element.7.direct, bf16[5,2,672,128]{3,2,1,0:T(8,128)(2,1)} %get-tuple-element.8.mirror), custom_call_target="tpu_custom_call" | custom-call | tf_op jit(solution)/shard_map/pallas_call | solution.py:568

commit v6 on v5

--- a/solution.py
+++ b/solution.py
@@ -102,27 +102,6 @@
     peers = (
         4 + jnp.where(crossing, 1, 0) + jnp.where(turned, 5, jnp.where(across, jnp.where(crossing, 6, 4), 2))
     )
-    pl.semaphore_wait(barrier, peers)
-
-    def remote(src, dst, send, recv, device):
-        return pltpu.make_async_remote_copy(
-            src_ref=src, dst_ref=dst, send_sem=send, recv_sem=recv, device_id=device, device_id_type=MESH
-        )
-
-    mine = pl.ds(chip * CHIP + c * HALF, HALF)
-    theirs = pl.ds(chip * CHIP + other * HALF, HALF)
-    own_w = [pltpu.make_async_copy(integ.at[:, c * HALF + j], wv.at[j, mine], own_sem.at[j]) for j in range(HALF)]
-    pair_w = [
-        remote(integ.at[:, other * HALF + j], wv.at[j, mine], pair_send.at[j], pair_recv.at[j], sibling)
-        for j in range(HALF)
-    ]
-    for j in range(HALF):
-        own_w[j].start()
-        pair_w[j].start()
-
-    mask_pair = remote(mine_v.at[other], mv, m_sem.at[0], m_sem.at[1], sibling)
-    mask_own = pltpu.make_async_copy(mine_v.at[c], ms.at[c], m_sem.at[2])
-
     def make_mask():
         count_rows = counts[...]
         slots = lists.shape[2]
@@ -138,6 +117,28 @@
                 live = jnp.where(kept[:, s : s + 1] == labels, 1.0, live)
             for half in range(2):
                 mine_v[half, i * 8 : i * 8 + HALF] = live[half * HALF : (half + 1) * HALF]
+
+    make_mask()
+    pl.semaphore_wait(barrier, peers)
+
+    def remote(src, dst, send, recv, device):
+        return pltpu.make_async_remote_copy(
+            src_ref=src, dst_ref=dst, send_sem=send, recv_sem=recv, device_id=device, device_id_type=MESH
+        )
+
+    mine = pl.ds(chip * CHIP + c * HALF, HALF)
+    theirs = pl.ds(chip * CHIP + other * HALF, HALF)
+    own_w = [pltpu.make_async_copy(integ.at[:, c * HALF + j], wv.at[j, mine], own_sem.at[j]) for j in range(HALF)]
+    pair_w = [
+        remote(integ.at[:, other * HALF + j], wv.at[j, mine], pair_send.at[j], pair_recv.at[j], sibling)
+        for j in range(HALF)
+    ]
+    for j in range(HALF):
+        own_w[j].start()
+        pair_w[j].start()
+
+    mask_pair = remote(mine_v.at[other], mv, m_sem.at[0], m_sem.at[1], sibling)
+    mask_own = pltpu.make_async_copy(mine_v.at[c], ms.at[c], m_sem.at[2])
 
     def piece(part, j, dz, dy):
         view = pl.ds(block(dz, dy) * CHIP + (c if part == 0 else other) * HALF, HALF)
@@ -441,7 +442,6 @@
         t_local[i].start()
         t_pair[i].start()
     stage0(1)
-    make_mask()
     mask_pair.start()
     mask_own.start()
     stage1(0)

time: 134 us -> 134 us (level)
  no operation moved by 1% of the time
where the time goes in v6:
time: 134 us; the launch traced here: 133 us
  Pallas kernels  133 us (99%)
    pallas_call x1, Pallas kernels, on_device(): pl.pallas_call(kernel, out_shape=(tiles, jax.ShapeDtypeStruct((HALF, 2, P...  127 us
    pallas_call x1, Pallas kernels, on_device(): pl.pallas_call(finish, grid=(HALF,), out_shape=tiles, in_specs=[ten, pl.B...  6.22 us

profile of v6, /device:TPU:28, one launch (start us, length us, event | category | flops | bytes accessed | tf_op | source)
XLA Modules:
  0.0 133.3 jit_solution(12061338069283528609)
XLA Ops:
  0.0 127.1 %shard_map.46 = (f32[5,10,128,128]{3,2,1,0:T(8,128)}, bf16[5,2,672,128]{3,2,1,0:T(8,128)(2,1)}) custom-call(bf16[5,80,128,128]{3,2,1,0:T(8,128)(2,1)} %amp.1, bf16[5,10,128,128]{3,2,1,0:T(8,128)(2,1)} %integ.1, s32[5,10,48]{2,1,0:T(8,128)} %lists.1, s32[5,10]{1,0:T(8,128)} %counts.1), custom_call_target="tpu_custom_call" | custom-call | flops 16999999488 | bytes 60000000 | tf_op jit(solution)/shard_map/pallas_call | solution.py:540
  127.1 6.2 %shard_map.47 = f32[5,10,128,128]{3,2,1,0:T(8,128)} custom-call(f32[5,10,128,128]{3,2,1,0:T(8,128)} %get-tuple-element.7.direct, bf16[5,2,672,128]{3,2,1,0:T(8,128)(2,1)} %get-tuple-element.8.mirror), custom_call_target="tpu_custom_call" | custom-call | tf_op jit(solution)/shard_map/pallas_call | solution.py:568
